TPU v7x, 128 devices: a whole 4x4x4 slice. The times are simulated.
128 devices in a mesh: row: 8 (over x, core), col: 16 (over y, z).
Axes of the slice: x: 4, y: 4, z: 4, core: 2. Of those that a mesh axis runs over, the one named last changes fastest.
Arguments:
- grad: float32 [16384, 1024], P('col', 'row'), may hold values from -6 to 6
- moment: float32 [16384, 1024], P('col', 'row'), may hold values from -6 to 6
- second: float32 [16384, 1024], P(('row', 'col')), may hold values from 1 to 10
- left_basis: float32 [16384, 16384], P('col', 'row'), as said below
- right_basis: float32 [1024, 1024], replicated, may hold values from -0.1875 to 0.1875
Outputs:
- update: float32 [16384, 1024], P('col', 'row')
- moment_new: float32 [16384, 1024], P('col', 'row')
- second_new: float32 [16384, 1024], P(('row', 'col'))
Inputs may be any that keep to these rules, and one draw needn't show every extreme that they name: left_basis is a dense real matrix whose columns have length close to one.
All inputs are finite; a program needn't handle non-finite values.
Results may differ from a plain program's by a relative error of at most 0.00007.
Values sent between devices are 32-bit elements; how exact they have to be, the bound alone decides.
No kernel may reach another device: no remote copies, remote signals or barrier semaphores. Data moves between devices by JAX's collectives and lax.ppermute only.
A program may use at most 128 MiB of HBM per device.

v0:
```python
import jax
import jax.numpy as jnp
from jax import lax
from jax.sharding import PartitionSpec as P

M = 16384
N = 1024


first_decay = 0.9
second_decay = 0.95
epsilon = 1e-08
clip_share = 0.25


def local(grad, moment, second, left_basis, right_basis):
    highest = lax.Precision.HIGHEST
    moment_new = first_decay * moment + (1.0 - first_decay) * grad
    stacked = jnp.stack([grad, moment_new], axis=0)
    partial_sums = jnp.einsum(
        "ki,skw->siw",
        left_basis,
        lax.all_gather(stacked, "row", axis=2, tiled=True),
        precision=highest,
    )
    partial_sums = jnp.einsum("sij,jn->sin", partial_sums, right_basis, precision=highest)
    shares = lax.psum_scatter(partial_sums, "col", scatter_dimension=1, tiled=True)
    grad_rot = shares[0]
    mom_rot = shares[1]
    second_new = second_decay * second + (1.0 - second_decay) * grad_rot * grad_rot
    rotated = mom_rot / (jnp.sqrt(second_new) + epsilon)
    total = lax.psum(jnp.sum(rotated * rotated), ("row", "col"))
    factor = jnp.minimum(1.0, clip_share * jnp.sqrt(jnp.float32(M * N)) / (jnp.sqrt(total) + 1e-06))
    rotated = rotated * factor
    back = lax.dot_general(rotated, right_basis, (((1,), (1,)), ((), ())), precision=highest)
    block_rows = lax.all_gather(back, "col", axis=0, tiled=True)
    flipped = lax.psum_scatter(
        lax.dot_general(block_rows, left_basis, (((0,), (1,)), ((), ())), precision=highest),
        "row",
        scatter_dimension=0,
        tiled=True,
    )
    update = flipped.T
    return (update, moment_new, second_new)


def solution(mesh):
    return jax.shard_map(
        local,
        mesh=mesh,
        in_specs=(P("col", "row"), P("col", "row"), P(("row", "col"), None), P("col", "row"), P()),
        out_specs=(P("col", "row"), P("col", "row"), P(("row", "col"), None)),
        check_vma=False,
    )
```

profile of v0, /device:TPU:0, one launch (start us, length us, event | category | flops | bytes accessed | tf_op | source)
XLA Modules:
  0.0 556.8 jit_solution(5209853239867363458)
XLA Ops:
  7.2 0.0 all-gather.3.cloned.1.call-start
  7.2 1.3 multiply_add_fusion
  8.5 0.0 copy-start.2
  8.5 2.3 pad_maximum_fusion
  10.8 0.0 all-gather.3.cloned.1.call-update
  10.8 0.0 reduce-scatter.3.cloned.1.call-start
  10.9 56.5 %all-gather.3.cloned.1.call-done = f32[2,1024,1024]{2,1,0:T(8,128)} async-done(((f32[2,1024,128]{2,1,0:T(8,128)}), f32[2,1024,1024]{2,1,0:T(8,128)}) %all-gather.3.cloned.1.call-update) | async-done | bytes 8388624 | tf_op jit(solution)/shard_map/all_gather | solution.py:23
  67.3 0.0 copy-start
  67.3 71.5 %fusion.2 = f32[2,1024,2048]{1,2,0:T(8,128)} fusion(f32[2,1024,1024]{2,1,0:T(8,128)} %all-gather.3.cloned.1.call-done, f32[1024,2048]{1,0:T(8,128)} %param.8), kind=kOutput, calls=%fused_computation.2 | convolution fusion | flops 51539607552 | bytes 33554432 | tf_op jit(solution)/shard_map/ki,skw->siw/dot_general | solution.py:20
  138.8 0.0 copy-done.2
  138.9 0.0 copy-done
  138.9 59.2 %fusion = f32[2,2048,1024]{2,1,0:T(8,128)} fusion(f32[2,1024,2048]{1,2,0:T(8,128)} %fusion.2, f32[1024,1024]{1,0:T(8,128)S(1)} %copy-done), kind=kOutput, calls=%fused_computation | convolution fusion | flops 51539607552 | bytes 37748736 | tf_op jit(solution)/shard_map/sij,jn->sin/dot_general | solution.py:26
  198.0 0.0 copy-start.3
  198.0 0.0 reduce-scatter.3.cloned.1.call-update
  198.0 0.0 all-gather.5.cloned.1.call-start
  198.1 111.8 %reduce-scatter.3.cloned.1.call-done = f32[2,128,1024]{2,1,0:T(8,128)} async-done(((f32[2,2048,1024]{2,1,0:T(8,128)}), f32[2,128,1024]{2,1,0:T(8,128)}) %reduce-scatter.3.cloned.1.call-update) | async-done | bytes 1048592 | tf_op jit(solution)/shard_map/reduce_scatter | solution.py:27
  309.9 0.0 copy-done.3
  309.9 2.1 multiply_reduce_fusion
  312.0 0.0 copy-start.1
  312.0 64.3 %psum.7 = f32[]{:T(128)} all-reduce(f32[]{:T(128)} %get-tuple-element.6), channel_id=1, replica_groups=mesh['row'=8,'col'=16] {'row','col'}, use_global_device_ids=true, to_apply=%region_2.0 | all-reduce | flops 1 | bytes 8 | tf_op jit(solution)/shard_map/psum | solution.py:32
  377.1 7.6 %fusion.7 = f32[128,1024]{1,0:T(8,128)} fusion(f32[1024,1024]{1,0:T(8,128)} %param.9, f32[]{:T(128)S(6)} %min_shard_map.3, f32[2,128,1024]{2,1,0:T(8,128)} %reduce-scatter.3.cloned.1.call-done, f32[128,1024]{1,0:T(8,128)S(1)} %get-tuple-element.7), kind=kOutput, calls=%fused_computation.11 | convolution fusion | flops 1611005952 | bytes 5767172 | tf_op jit(solution)/shard_map/dot_general | solution.py:35
  384.7 0.0 all-gather.5.cloned.1.call-update
  384.7 0.0 reduce-scatter.5.cloned.1.call-start
  384.7 68.3 %all-gather.5.cloned.1.call-done = f32[2048,1024]{1,0:T(8,128)} async-done(((f32[128,1024]{1,0:T(8,128)}), f32[2048,1024]{1,0:T(8,128)}) %all-gather.5.cloned.1.call-update) | async-done | bytes 8388624 | tf_op jit(solution)/shard_map/all_gather | solution.py:36
  453.0 57.2 %fusion.12 = f32[1024,1024]{1,0:T(8,128)} fusion(f32[2048,1024]{1,0:T(8,128)} %all-gather.5.cloned.1.call-done, f32[1024,2048]{1,0:T(8,128)} %param.8), kind=kOutput, calls=%fused_computation.16 | convolution fusion | flops 25769803776 | bytes 20971520 | tf_op jit(solution)/shard_map/dot_general | solution.py:38
  510.2 0.0 copy-done.1
  510.2 0.0 reduce-scatter.5.cloned.1.call-update
  510.3 37.6 %reduce-scatter.5.cloned.1.call-done = f32[128,1024]{1,0:T(8,128)} async-done(((f32[1024,1024]{1,0:T(8,128)}), f32[128,1024]{1,0:T(8,128)}) %reduce-scatter.5.cloned.1.call-update) | async-done | bytes 524304 | tf_op jit(solution)/shard_map/reduce_scatter | solution.py:37
  547.8 2.0 copy.8
Async XLA Ops:
  7.2 60.2 %all-gather.3.cloned.1.call-start = ((), (), s32[]{:S(2)}) async-start(), calls=%async_computation.2 | async-start | bytes 9437184 | tf_op jit(solution)/shard_map/all_gather | solution.py:23
  8.5 130.3 %copy-start.2 = (f32[1024,128]{1,0:T(8,128)}, f32[1024,128]{1,0:T(8,128)S(1)}, u32[]{:S(2)}) copy-start(f32[1024,128]{1,0:T(8,128)S(1)} %multiply_add_fusion) | copy-start | bytes 1572868
  10.8 299.1 %reduce-scatter.3.cloned.1.call-start = ((), (), s32[]{:S(2)}) async-start(), calls=%async_computation.3 | async-start | bytes 17825792 | tf_op jit(solution)/shard_map/reduce_scatter | solution.py:27
  67.3 71.5 %copy-start = (f32[1024,1024]{1,0:T(8,128)S(1)}, f32[1024,1024]{1,0:T(8,128)}, u32[]{:S(2)}) copy-start(f32[1024,1024]{1,0:T(8,128)} %param.9) | copy-start | bytes 12582916
  198.0 111.9 %copy-start.3 = (f32[128,1024]{1,0:T(8,128)S(1)}, f32[128,1024]{1,0:T(8,128)}, u32[]{:S(2)}) copy-start(f32[128,1024]{1,0:T(8,128)} %param.7) | copy-start | bytes 1572868
  198.0 255.0 %all-gather.5.cloned.1.call-start = ((), (), s32[]{:S(2)}) async-start(), calls=%async_computation.4 | async-start | bytes 8912896 | tf_op jit(solution)/shard_map/all_gather | solution.py:36
  312.0 198.2 %copy-start.1 = (f32[128,1024]{1,0:T(8,128)}, f32[128,1024]{1,0:T(8,128)S(1)}, u32[]{:S(2)}) copy-start(f32[128,1024]{1,0:T(8,128)S(1)} %get-tuple-element.7) | copy-start | bytes 1572868
  384.7 163.1 %reduce-scatter.5.cloned.1.call-start = ((), (), s32[]{:S(2)}) async-start(), calls=%async_computation.5 | async-start | bytes 4718592 | tf_op jit(solution)/shard_map/reduce_scatter | solution.py:37
Sparse Core Ops, SparseCore 0:
  10.9 56.3 all-gather.2
  198.2 111.7 reduce-scatter.2
  384.8 68.1 all-gather.4
  510.4 37.4 reduce-scatter.4
where the time goes:
time: 567 us; the launch traced here: 557 us
  waiting for transfers between devices  274 us (48%)
  matrix products  195 us (34%)
  blocking collectives  64.3 us (11%)
  between operations  14.9 us (3%)
    reduce_scatter x1, waiting for transfers between devices, local(): lax.psum_scatter(partial_sums, 'col', scatter_dimension=1, tiled=True)  112 us
    dot_general x1, matrix products, local(): jnp.einsum('ki,skw->siw', left_basis, lax.all_gather(stacked, 'row', axis...  71.5 us
    all_gather x1, waiting for transfers between devices, local(): block_rows = lax.all_gather(back, 'col', axis=0, tiled=True)  68.3 us
    psum x1, blocking collectives, local(): total = lax.psum(jnp.sum(rotated * rotated), ('row', 'col'))  64.3 us
    dot_general x1, matrix products, local(): jnp.einsum('sij,jn->sin', partial_sums, right_basis, precision=highest)  59.2 us
    dot_general x1, matrix products, local(): lax.dot_general(block_rows, left_basis, (((0,), (1,)), ((), ())), precisi...  57.2 us
    all_gather x1, waiting for transfers between devices, local(): lax.all_gather(stacked, 'row', axis=2, tiled=True)  56.5 us
    reduce_scatter x1, waiting for transfers between devices, local(): lax.psum_scatter(lax.dot_general(block_rows, left_basis, (((0,), (1,)), (...  37.6 us
  transfers between devices with their start and end apart: 4, of which 4 were waited for; matrix products, arithmetic and copies ran while one was open for 0% of the time, Pallas kernels for 0%

commit v1 on v0

v1 whole, which is shorter than its diff:
```python
import jax
import jax.numpy as jnp
from jax import lax
from jax.sharding import PartitionSpec as P

M = 16384
N = 1024


first_decay = 0.9
second_decay = 0.95
epsilon = 1e-08
clip_share = 0.25


def total_over_devices(value):
    for axis, size in (("row", 8), ("col", 16)):
        bit = 1
        while bit < size:
            value = value + lax.ppermute(value, axis, [(i, i ^ bit) for i in range(size)])
            bit *= 2
    return value


def local(grad, moment, second, left_basis, right_basis):
    high = lax.Precision.HIGH
    moment_new = first_decay * moment + (1.0 - first_decay) * grad
    stacked = jnp.stack([grad, moment_new], axis=0)
    partial_sums = jnp.einsum(
        "ki,skw->siw",
        left_basis,
        lax.all_gather(stacked, "row", axis=2, tiled=True),
        precision=high,
    )
    shares = lax.psum_scatter(partial_sums, "col", scatter_dimension=1, tiled=True)
    shares = jnp.einsum("sij,jn->sin", shares, right_basis, precision=high)
    grad_rot = shares[0]
    mom_rot = shares[1]
    second_new = second_decay * second + (1.0 - second_decay) * grad_rot * grad_rot
    rotated = mom_rot / (jnp.sqrt(second_new) + epsilon)
    back = lax.dot_general(rotated, right_basis, (((1,), (1,)), ((), ())), precision=high)
    block_rows = lax.all_gather(back, "col", axis=0, tiled=True)
    squares = jnp.sum((rotated * rotated).reshape(16, 8, 8, 128), axis=(0, 2))
    total = jnp.sum(total_over_devices(squares))
    factor = jnp.minimum(1.0, clip_share * jnp.sqrt(jnp.float32(M * N)) / (jnp.sqrt(total) + 1e-06))
    flipped = lax.psum_scatter(
        lax.dot_general(block_rows, left_basis, (((0,), (1,)), ((), ())), precision=high),
        "row",
        scatter_dimension=0,
        tiled=True,
    )
    update = flipped.T * factor
    return (update, moment_new, second_new)


def solution(mesh):
    return jax.shard_map(
        local,
        mesh=mesh,
        in_specs=(P("col", "row"), P("col", "row"), P(("row", "col"), None), P("col", "row"), P()),
        out_specs=(P("col", "row"), P("col", "row"), P(("row", "col"), None)),
        check_vma=False,
    )
```

time: 567 us -> 370 us (0.65); the launches traced: 557 us -> 370 us
  matrix products: 195 us -> 73.4 us
  blocking collectives: 64.3 us -> 0 us
  starting transfers between devices: 0.16 us -> 13.5 us
  waiting for transfers between devices: 274 us -> 262 us
    psum x1 -> x0, blocking collectives: 64.3 us -> none  [local(): total = lax.psum(jnp.sum(rotated * rotated), ('row', 'col'))]
    dot_general x1, matrix products: 59.2 us -> 4.68 us  [local(): shares = jnp.einsum('sij,jn->sin', shares, right_basis, precision=high)]
    dot_general x1, matrix products: 71.5 us -> 33.3 us  [local(): jnp.einsum('ki,skw->siw', left_basis, lax.all_gather(stacked, 'row', axis...]
    reduce_scatter x1, waiting for transfers between devices: 37.6 us -> 8.89 us  [local(): lax.psum_scatter(lax.dot_general(block_rows, left_basis, (((0,), (1,)), (...]
    dot_general x1, matrix products: 57.2 us -> 32.4 us  [local(): lax.dot_general(block_rows, left_basis, (((0,), (1,)), ((), ())), precisi...]
    ppermute x0 -> x7, waiting for transfers between devices: none -> 14.1 us  [total_over_devices(): lax.ppermute(value, axis, [(i, i ^ bit) for i in range(size)])]
    ppermute x0 -> x7, starting transfers between devices: none -> 13.3 us  [total_over_devices(): lax.ppermute(value, axis, [(i, i ^ bit) for i in range(size)])]
  transfers between devices with their start and end apart: 4 -> 11, of which waited for: 4 -> 11; matrix products, arithmetic and copies ran while one was open for 0% -> 0% of each run, Pallas kernels for 0% -> 0%
where the time goes in v1:
time: 370 us
  waiting for transfers between devices  262 us (71%)
  matrix products  73.4 us (20%)
  between operations  14.6 us (4%)
  starting transfers between devices  13.5 us (4%)
  other arithmetic  5.55 us (2%)
    reduce_scatter x1, waiting for transfers between devices, local(): lax.psum_scatter(partial_sums, 'col', scatter_dimension=1, tiled=True)  112 us
    all_gather x1, waiting for transfers between devices, local(): block_rows = lax.all_gather(back, 'col', axis=0, tiled=True)  70.4 us
    all_gather x1, waiting for transfers between devices, local(): lax.all_gather(stacked, 'row', axis=2, tiled=True)  56.5 us
    dot_general x1, matrix products, local(): jnp.einsum('ki,skw->siw', left_basis, lax.all_gather(stacked, 'row', axis...  33.3 us
    dot_general x1, matrix products, local(): lax.dot_general(block_rows, left_basis, (((0,), (1,)), ((), ())), precisi...  32.4 us
    ppermute x7, waiting for transfers between devices, total_over_devices(): lax.ppermute(value, axis, [(i, i ^ bit) for i in range(size)])  14.1 us
    ppermute x7, starting transfers between devices, total_over_devices(): lax.ppermute(value, axis, [(i, i ^ bit) for i in range(size)])  13.3 us
    reduce_scatter x1, waiting for transfers between devices, local(): lax.psum_scatter(lax.dot_general(block_rows, left_basis, (((0,), (1,)), (...  8.89 us
  transfers between devices with their start and end apart: 11, of which 11 were waited for; matrix products, arithmetic and copies ran while one was open for 0% of the time, Pallas kernels for 0%

profile of v1, /device:TPU:0, one launch (start us, length us, event | category | flops | bytes accessed | tf_op | source)
XLA Modules:
  0.0 369.7 jit_solution(14086573079747252516)
XLA Ops:
  7.2 0.0 all-gather.3.cloned.1.call-start
  7.2 1.3 multiply_add_fusion
  8.5 0.0 copy-start.1
  8.5 2.3 pad_maximum_fusion
  10.8 0.0 all-gather.3.cloned.1.call-update
  10.8 0.0 reduce-scatter.3.cloned.1.call-start
  10.9 56.5 %all-gather.3.cloned.1.call-done = f32[2,1024,1024]{2,1,0:T(8,128)} async-done(((f32[2,1024,128]{2,1,0:T(8,128)}), f32[2,1024,1024]{2,1,0:T(8,128)}) %all-gather.3.cloned.1.call-update) | async-done | bytes 8388624 | tf_op jit(solution)/shard_map/all_gather | solution.py:32
  67.3 33.3 %fusion.2 = f32[2,2048,1024]{2,1,0:T(8,128)} fusion(f32[2,1024,1024]{2,1,0:T(8,128)} %all-gather.3.cloned.1.call-done, f32[1024,2048]{1,0:T(8,128)} %param.8), kind=kOutput, calls=%fused_computation.2 | convolution fusion | flops 25769803776 | bytes 33554432 | tf_op jit(solution)/shard_map/ki,skw->siw/dot_general | solution.py:29
  100.6 0.0 copy-done.1
  100.6 0.0 copy-start.3
  100.6 0.0 reduce-scatter.3.cloned.1.call-update
  100.6 0.0 all-gather.5.cloned.1.call-start
  100.7 111.8 %reduce-scatter.3.cloned.1.call-done = f32[2,128,1024]{2,1,0:T(8,128)} async-done(((f32[2,2048,1024]{2,1,0:T(8,128)}), f32[2,128,1024]{2,1,0:T(8,128)}) %reduce-scatter.3.cloned.1.call-update) | async-done | bytes 1048592 | tf_op jit(solution)/shard_map/reduce_scatter | solution.py:35
  212.5 0.0 copy-start
  212.5 4.7 %fusion.5 = f32[2,128,1024]{2,1,0:T(8,128)S(1)} fusion(f32[2,128,1024]{2,1,0:T(8,128)} %reduce-scatter.3.cloned.1.call-done, f32[1024,1024]{1,0:T(8,128)} %param.9), kind=kOutput, calls=%fused_computation.3 | convolution fusion | flops 1610612736 | bytes 6291456 | tf_op jit(solution)/shard_map/sij,jn->sin/dot_general | solution.py:36
  217.2 0.0 copy-done.3
  217.2 0.3 bitcast_reduce_fusion
  217.5 0.0 copy-start.2
  217.5 0.0 copy-done
  217.5 3.1 fusion.9
  220.6 0.0 all-gather.5.cloned.1.call-update
  220.6 0.0 reduce-scatter.5.cloned.1.call-start
  220.7 70.4 %all-gather.5.cloned.1.call-done = f32[2048,1024]{1,0:T(8,128)} async-done(((f32[128,1024]{1,0:T(8,128)}), f32[2048,1024]{1,0:T(8,128)}) %all-gather.5.cloned.1.call-update) | async-done | bytes 8388624 | tf_op jit(solution)/shard_map/all_gather | solution.py:42
  291.1 32.4 %fusion.12 = f32[1024,1024]{1,0:T(8,128)} fusion(f32[2048,1024]{1,0:T(8,128)} %all-gather.5.cloned.1.call-done, f32[1024,2048]{1,0:T(8,128)} %param.8), kind=kOutput, calls=%fused_computation.16 | convolution fusion | flops 12884901888 | bytes 20971520 | tf_op jit(solution)/shard_map/dot_general | solution.py:47
  323.4 0.0 copy-done.2
  323.4 0.0 reduce-scatter.5.cloned.1.call-update
  323.5 0.1 collective-permute-start
  323.6 1.2 collective-permute-done
  324.7 1.5 collective-permute-start.1
  326.2 2.1 collective-permute-done.1
  328.3 3.0 collective-permute-start.2
  331.3 2.1 collective-permute-done.2
  333.4 1.3 collective-permute-start.3
  334.8 2.3 collective-permute-done.3
  337.1 2.9 collective-permute-start.4
  340.0 2.2 collective-permute-done.4
  342.2 1.5 collective-permute-start.5
  343.7 2.1 collective-permute-done.5
  345.8 3.0 collective-permute-start.6
  348.8 2.1 collective-permute-done.6
  350.9 0.6 add_reduce_fusion
  352.2 8.9 %reduce-scatter.5.cloned.1.call-done = f32[128,1024]{1,0:T(8,128)} async-done(((f32[1024,1024]{1,0:T(8,128)}), f32[128,1024]{1,0:T(8,128)}) %reduce-scatter.5.cloned.1.call-update) | async-done | bytes 524304 | tf_op jit(solution)/shard_map/reduce_scatter | solution.py:46
  361.1 1.1 multiply_bitcast_fusion
  362.2 1.0 copy.9
  (6 shorter events, 0.0 us)
Async XLA Ops:
  7.2 60.2 %all-gather.3.cloned.1.call-start = ((), (), s32[]{:S(2)}) async-start(), calls=%async_computation.2 | async-start | bytes 9437184 | tf_op jit(solution)/shard_map/all_gather | solution.py:32
  8.5 92.1 %copy-start.1 = (f32[1024,128]{1,0:T(8,128)}, f32[1024,128]{1,0:T(8,128)S(1)}, u32[]{:S(2)}) copy-start(f32[1024,128]{1,0:T(8,128)S(1)} %multiply_add_fusion) | copy-start | bytes 1572868
  10.8 201.7 %reduce-scatter.3.cloned.1.call-start = ((), (), s32[]{:S(2)}) async-start(), calls=%async_computation.3 | async-start | bytes 17825792 | tf_op jit(solution)/shard_map/reduce_scatter | solution.py:35
  100.6 116.6 %copy-start.3 = (f32[128,1024]{1,0:T(8,128)S(1)}, f32[128,1024]{1,0:T(8,128)}, u32[]{:S(2)}) copy-start(f32[128,1024]{1,0:T(8,128)} %param.7) | copy-start | bytes 1572868
  100.6 190.5 %all-gather.5.cloned.1.call-start = ((), (), s32[]{:S(2)}) async-start(), calls=%async_computation.4 | async-start | bytes 8912896 | tf_op jit(solution)/shard_map/all_gather | solution.py:42
  212.5 5.0 %copy-start = (f32[1024,1024]{1,0:T(8,128)S(1)}, f32[1024,1024]{1,0:T(8,128)}, u32[]{:S(2)}) copy-start(f32[1024,1024]{1,0:T(8,128)} %param.9) | copy-start | bytes 12582916
  217.5 106.0 %copy-start.2 = (f32[128,1024]{1,0:T(8,128)}, f32[128,1024]{1,0:T(8,128)S(1)}, u32[]{:S(2)}) copy-start(f32[128,1024]{1,0:T(8,128)S(1)} %get-tuple-element.10) | copy-start | bytes 1572868
  220.6 140.5 %reduce-scatter.5.cloned.1.call-start = ((), (), s32[]{:S(2)}) async-start(), calls=%async_computation.5 | async-start | bytes 4718592 | tf_op jit(solution)/shard_map/reduce_scatter | solution.py:46
  323.5 1.2 collective-permute-start
  324.7 3.6 collective-permute-start.1
  328.3 5.1 %collective-permute-start.2 = (f32[8,128]{1,0:T(8,128)S(1)}, f32[8,128]{1,0:T(8,128)S(1)}, u32[]{:S(2)}, u32[]{:S(2)}) collective-permute-start(f32[8,128]{1,0:T(8,128)S(1)} %add.45), channel_id=1, source_target_pairs={{0,64},{16,80},{32,96},{48,112},{64,0},{80,16},{96,32},{112,48},{1... | collective-permute-start | bytes 12296 | tf_op jit(solution)/shard_map/ppermute | solution.py:20
  333.4 3.6 collective-permute-start.3
  337.1 5.1 %collective-permute-start.4 = (f32[8,128]{1,0:T(8,128)S(1)}, f32[8,128]{1,0:T(8,128)S(1)}, u32[]{:S(2)}, u32[]{:S(2)}) collective-permute-start(f32[8,128]{1,0:T(8,128)S(1)} %add.47), channel_id=1, source_target_pairs={{0,2},{1,3},{2,0},{3,1},{4,6},{5,7},{6,4},{7,5},{8,10},{9,11},{10,... | collective-permute-start | bytes 12296 | tf_op jit(solution)/shard_map/ppermute | solution.py:20
  342.2 3.6 collective-permute-start.5
  345.8 5.1 %collective-permute-start.6 = (f32[8,128]{1,0:T(8,128)S(1)}, f32[8,128]{1,0:T(8,128)S(1)}, u32[]{:S(2)}, u32[]{:S(2)}) collective-permute-start(f32[8,128]{1,0:T(8,128)S(1)} %add.49), channel_id=1, source_target_pairs={{0,8},{1,9},{2,10},{3,11},{4,12},{5,13},{6,14},{7,15},{8,0},{9,1},... | collective-permute-start | bytes 12296 | tf_op jit(solution)/shard_map/ppermute | solution.py:20
Sparse Core Ops, SparseCore 0:
  10.9 56.3 all-gather.2
  100.7 111.6 reduce-scatter.2
  220.8 70.2 all-gather.4
  323.6 37.4 reduce-scatter.4

commit v2 on v0

v2 whole, which is shorter than its diff:
```python
import functools

import jax
import jax.numpy as jnp
from jax import lax
from jax.experimental import pallas as pl
from jax.experimental.pallas import tpu as pltpu
from jax.sharding import PartitionSpec as P

M = 16384
N = 1024

first_decay = 0.9
second_decay = 0.95
epsilon = 1e-08
clip_share = 0.25

f32, bf16 = jnp.float32, jnp.bfloat16
BOTH = ("row", "col")
VMEM_LIMIT = 40 * 1024 * 1024


def call(kernel, grid, in_specs, out_specs, out_shape, scratch=(), flops=0, moved=0, aliases=None, prefetch=0, name=None):
    return pl.pallas_call(
        kernel,
        grid_spec=pltpu.PrefetchScalarGridSpec(
            num_scalar_prefetch=prefetch, grid=grid, in_specs=in_specs, out_specs=out_specs, scratch_shapes=list(scratch)
        ),
        out_shape=out_shape,
        input_output_aliases=aliases or {},
        compiler_params=pltpu.CompilerParams(vmem_limit_bytes=VMEM_LIMIT, dimension_semantics=("arbitrary",) * len(grid)),
        cost_estimate=pl.CostEstimate(flops=flops, bytes_accessed=moved, transcendentals=0),
        name=name,
    )


def shape(rows, columns, dtype=f32):
    return jax.ShapeDtypeStruct((rows, columns), dtype)


def split(value):
    high = value.astype(bf16)
    return high, (value - high.astype(f32)).astype(bf16)


def dot3(a_high, a_low, b_high, b_low, dims=(((1,), (0,)), ((), ()))):
    d = functools.partial(lax.dot_general, dimension_numbers=dims, preferred_element_type=f32)
    return d(a_high, b_high) + (d(a_high, b_low) + d(a_low, b_high))


def move(value, step):
    pairs = []
    for x in range(4):
        for c in range(2):
            for y in range(4):
                for z in range(4):
                    tx, tc, ty, tz = step(x, c, y, z)
                    pairs.append(((2 * x + c) * 16 + 4 * y + z, (2 * (tx % 4) + tc) * 16 + 4 * (ty % 4) + tz % 4))
    return lax.ppermute(value, BOTH, pairs)


def swap(value):
    return move(value, lambda x, c, y, z: (x, 1 - c, y, z))


def along_x(value, d):
    return move(value, lambda x, c, y, z: (x + d, c, y, z))


def first(value, d):
    return move(value, lambda x, c, y, z: (x, c, y + d, z) if c == 0 else (x, c, y, z + d))


def second_axis(value, d):
    return move(value, lambda x, c, y, z: (x, c, y, z + d) if c == 0 else (x, c, y + d, z))


def start(core, grad, moment):
    def kernel(core_ref, grad_ref, moment_ref, new_ref, keep_ref, give_ref):
        g = grad_ref[...]
        new = first_decay * moment_ref[...] + (1.0 - first_decay) * g
        new_ref[...] = new
        g, new = g.T, new.T
        zero = core_ref[0] == 0
        keep_ref[...] = jnp.where(zero, g, new)
        give_ref[...] = jnp.where(zero, new, g)

    block = pl.BlockSpec((256, 128), lambda t, c: (t, 0))
    turned = pl.BlockSpec((128, 256), lambda t, c: (0, t))
    return call(
        kernel, (4,), [block, block], [block, turned, turned], [shape(1024, 128), shape(128, 1024), shape(128, 1024)],
        moved=3 * 2**20, flops=10**6, prefetch=1, name="start",
    )(core, grad, moment)


def order_left(order, left, half, held=None):
    def kernel(order_ref, left_ref, *refs):
        high_ref, low_ref = refs[-2:]
        high, low = split(left_ref[...])
        high_ref[...] = high
        low_ref[...] = low

    out = pl.BlockSpec((1024, 128), lambda a, b, o: (0, a * 8 + half * 4 + b))
    anywhere = pl.BlockSpec(memory_space=pl.ANY)
    more = [] if held is None else list(held)
    return call(
        kernel, (4, 4), [pl.BlockSpec((1024, 128), lambda a, b, o: (0, o[a * 4 + b]))] + [anywhere] * len(more),
        [out, out], [shape(1024, 4096, bf16)] * 2, moved=16 * 2**20, flops=10**7,
        aliases={2: 0, 3: 1} if more else None, prefetch=1, name="order_left",
    )(order, left, *more)


def order_right(order, right):
    def kernel(order_ref, right_ref, high_ref, low_ref):
        high, low = split(right_ref[...])
        high_ref[...] = high
        low_ref[...] = low

    out = pl.BlockSpec((128, 1024), lambda a, o: (a, 0))
    return call(
        kernel, (8,), [pl.BlockSpec((128, 1024), lambda a, o: (o[a], 0))], [out, out], [shape(1024, 1024, bf16)] * 2,
        moved=8 * 2**20, flops=10**6, prefetch=1, name="order_right",
    )(order, right)


def project(blocks, left, d, more=None, side=0, halves=False):
    rows = sum(b.shape[0] for b in blocks)
    n = len(blocks)

    def kernel(*refs):
        g_refs, (lh, ll) = refs[:n], refs[n : n + 2]
        gh, gl = refs[-2:]
        outs = refs[n + 2 + (more is not None) : -2]
        t = pl.program_id(0)

        @pl.when(t == 0)
        def _():
            at = 0
            for g in g_refs:
                size = g.shape[0]
                gh[at : at + size, :], gl[at : at + size, :] = split(g[...])
                at += size

        value = dot3(gh[...], gl[...], lh[...], ll[...])
        if halves:

            @pl.when(t < 2)
            def _():
                outs[0][...] = value

            @pl.when(t >= 2)
            def _():
                outs[1][...] = value

        elif more is not None:
            here = t < 2 if side == 0 else t >= 2

            @pl.when(here)
            def _():
                outs[0][...] = value + refs[n + 2][...]

            @pl.when(jnp.logical_not(here))
            def _():
                outs[0][...] = value

        else:
            outs[0][...] = value

    column = pl.BlockSpec((1024, 256), lambda t: (0, d * 4 + t))
    in_specs = [pl.BlockSpec(b.shape, lambda t: (0, 0)) for b in blocks] + [column, column]
    args = list(blocks) + list(left)
    low = pl.BlockSpec((rows, 256), lambda t: (0, jnp.minimum(t, 1)))
    high = pl.BlockSpec((rows, 256), lambda t: (0, jnp.maximum(t - 2, 0)))
    if more is not None:
        in_specs.append(high if side else low)
        args.append(more)
    if halves:
        out_specs, out_shape = [low, high], [shape(rows, 512)] * 2
    else:
        out_specs, out_shape = pl.BlockSpec((rows, 256), lambda t: (0, t)), shape(rows, 1024)
    return call(
        kernel, (4,), in_specs, out_specs, out_shape, [pltpu.VMEM((rows, 1024), bf16)] * 2,
        flops=6 * rows * 2**20, moved=4 * 2**20 + rows * 8192, name=f"project{d}",
    )(*args)


def settle(own, one, two):
    rows = own.shape[0]

    def kernel(a, b, c, *outs):
        value = a[...] + b[...] + c[...]
        for d, out in enumerate(outs):
            out[:, :128] = value[:, d * 128 : d * 128 + 128]
            out[:, 128:] = value[:, 512 + d * 128 : 640 + d * 128]

    block = pl.BlockSpec((128, 1024), lambda t: (t, 0))
    return call(
        kernel, (rows // 128,), [block] * 3, [pl.BlockSpec((128, 256), lambda t: (t, 0))] * 4, [shape(rows, 256)] * 4,
        flops=2 * rows * 1024, moved=rows * 16384, name="settle",
    )(own, one, two)


def rotate(parts, right, chips, before=None):
    rows = parts[0].shape[0]
    last = before is not None

    def kernel(*refs):
        p, (rh, rl) = refs[:4], refs[4:6]
        th, tl = refs[-2:]
        t = pl.program_id(0)

        @pl.when(t == 0)
        def _():
            total = (p[0][...] + p[1][...]) + (p[2][...] + p[3][...])
            th[...], tl[...] = split(total.T)

        def pick(r):
            return jnp.concatenate([r[h * 512 + d * 128 : h * 512 + d * 128 + 128, :] for d in chips for h in range(2)], axis=0)

        value = dot3(th[...], tl[...], pick(rh), pick(rl))
        if last:
            value = value + refs[6][...]
            refs[7][...] = value[:128]
            refs[8][...] = value[128:]
        else:
            refs[6][...] = value

    part = pl.BlockSpec((rows, 256), lambda t: (0, 0))
    column = pl.BlockSpec((1024, 256), lambda t: (0, t))
    tall = pl.BlockSpec((256, 256), lambda t: (0, t))
    flat = pl.BlockSpec((128, 256), lambda t: (0, t))
    return call(
        kernel, (4,), [part] * 4 + [column] * 2 + ([tall] if last else []),
        [flat, flat] if last else tall, [shape(128, 1024)] * 2 if last else shape(256, 1024),
        [pltpu.VMEM((256, rows), bf16)] * 2, flops=6 * 256 * rows * 1024, moved=8 * 2**20, name="rotate",
    )(*parts, *right, *([before] if last else []))


def turn(core, own, other, second, right):
    def kernel(core_ref, own_ref, other_ref, second_ref, rh, rl, new_ref, keep_ref, give_ref, sum_ref, th, tl):
        t = pl.program_id(0)

        @pl.when(t == 0)
        def _():
            zero = core_ref[0] == 0
            a, b = own_ref[...], other_ref[...]
            g, m = jnp.where(zero, a, b), jnp.where(zero, b, a)
            new = second_decay * second_ref[...] + (1.0 - second_decay) * g * g
            new_ref[...] = new
            rotated = m / (jnp.sqrt(new) + epsilon)
            th[...], tl[...] = split(rotated)
            squares = rotated * rotated
            total = squares[0:8, :]
            for i in range(1, 16):
                total = total + squares[i * 8 : i * 8 + 8, :]
            narrow = total[:, 0:128]
            for i in range(1, 8):
                narrow = narrow + total[:, i * 128 : i * 128 + 128]
            sum_ref[...] = narrow

        value = dot3(th[...], tl[...], rh[...], rl[...], (((1,), (1,)), ((), ())))

        @pl.when(t < 2)
        def _():
            keep_ref[...] = value

        @pl.when(t >= 2)
        def _():
            give_ref[...] = value

    whole = pl.BlockSpec((128, 1024), lambda t, c: (0, 0))
    rows = pl.BlockSpec((256, 1024), lambda t, c: (t, 0))
    return call(
        kernel, (4,), [whole, whole, whole, rows, rows],
        [
            whole,
            pl.BlockSpec((128, 256), lambda t, c: (0, jnp.minimum(t, 1))),
            pl.BlockSpec((128, 256), lambda t, c: (0, jnp.maximum(t - 2, 0))),
            pl.BlockSpec((8, 128), lambda t, c: (0, 0)),
        ],
        [shape(128, 1024), shape(128, 512), shape(128, 512), shape(8, 128)],
        [pltpu.VMEM((128, 1024), bf16)] * 2, flops=6 * 128 * 2**20, moved=7 * 2**20, prefetch=1, name="turn",
    )(core, own, other, second, *right)


def back_project(terms, left, before=None, cut=False):
    arrays = [a for _, group in terms for a in group]
    n, g = len(arrays), len(terms)

    def kernel(*refs):
        s_refs, l_refs = refs[:n], refs[n : n + 2 * g]
        sh, sl = refs[-2:]
        outs = refs[n + 2 * g + (before is not None) : -2]
        t = pl.program_id(0)

        @pl.when(t == 0)
        def _():
            at = 0
            for s in s_refs:
                size = s.shape[0]
                sh[at : at + size, :], sl[at : at + size, :] = split(s[...])
                at += size

        value = refs[n + 2 * g][...] if before is not None else None
        for i in range(g):
            rows = slice(i * 1024, i * 1024 + 1024)
            new = dot3(l_refs[2 * i][...], l_refs[2 * i + 1][...], sh[rows, :], sl[rows, :])
            value = new if value is None else value + new
        if cut:
            for d, out in enumerate(outs):
                out[...] = value[:, d * 128 : d * 128 + 128]
        else:
            outs[0][...] = value

    wide = pl.BlockSpec((256, 512), lambda t: (t, 0))
    in_specs = [pl.BlockSpec(a.shape, lambda t: (0, 0)) for a in arrays]
    args = list(arrays)
    for d, _ in terms:
        in_specs += [pl.BlockSpec((256, 1024), lambda t, d=d: (t, d))] * 2
        args += list(left)
    if before is not None:
        in_specs.append(wide)
        args.append(before)
    if cut:
        out_specs, out_shape = [pl.BlockSpec((256, 128), lambda t: (t, 0))] * 4, [shape(1024, 128)] * 4
    else:
        out_specs, out_shape = wide, shape(1024, 512)
    return call(
        kernel, (4,), in_specs, out_specs, out_shape, [pltpu.VMEM((1024 * g, 512), bf16)] * 2,
        flops=6 * g * 2**29, moved=(6 * g + 4) * 2**20, name="back_project",
    )(*args)


def scatter_sum(blocks, left):
    two_a, two_b = project(blocks, left, 2, halves=True)
    near = first(two_a, 1)
    far = first(two_b, -1)
    own = project(blocks, left, 0)
    up = first(project(blocks, left, 1, near, 0), 1)
    down = first(project(blocks, left, 3, far, 1), -1)
    q = settle(own, up, down)
    return [q[0], second_axis(q[1], 1), second_axis(q[3], -1), second_axis(q[2], 2)]


def local(grad, moment, second, left_basis, right_basis):
    row, col = lax.axis_index("row"), lax.axis_index("col")
    x, c, y, z = row // 2, row % 2, col // 4, col % 4
    core = c.reshape(1).astype(jnp.int32)
    a, b = jnp.arange(4)[:, None], jnp.arange(4)[None, :]
    u, v = jnp.where(c == 0, y, z), jnp.where(c == 0, z, y)
    u, v = (u + a) % 4, (v + b) % 4
    order = jnp.where(c == 0, u * 4 + v, v * 4 + u).reshape(16).astype(jnp.int32)
    halves, chips = jnp.arange(2)[:, None], jnp.arange(4)[None, :]
    order_r = (2 * ((x + chips) % 4) + (c + halves) % 2).reshape(8).astype(jnp.int32)

    moment_new, keep, give = start(core, grad, moment)
    mine = jnp.concatenate([keep, swap(give)], axis=0)
    left_other = swap(left_basis)
    plus = along_x(mine, -1)
    minus = along_x(mine, 1)
    left = order_left(order, left_basis, 0)
    right = order_right(order_r, right_basis)
    left = order_left(order, left_other, 1, left)
    far_a = along_x(plus[:128], -1)
    far_b = along_x(minus[128:], 1)

    z0 = scatter_sum([mine, plus], left)
    z1 = scatter_sum([minus, far_a, far_b], left)
    part = rotate(z0, right, (0, 1))
    own, other = rotate(z1, right, (3, 2), part)
    other = swap(other)

    second_new, keep, give, squares = turn(core, own, other, second, right)
    share = jnp.stack([keep, swap(give)], axis=0)
    for step in (
        lambda x, c, y, z: (x, 1 - c, y, z),
        lambda x, c, y, z: (x ^ 1, c, y, z),
        lambda x, c, y, z: (x ^ 2, c, y, z),
        lambda x, c, y, z: (x, c, y ^ 1, z),
        lambda x, c, y, z: (x, c, y ^ 2, z),
        lambda x, c, y, z: (x, c, y, z ^ 1),
        lambda x, c, y, z: (x, c, y, z ^ 2),
    ):
        squares = squares + move(squares, step)
    total = jnp.sum(squares)
    factor = jnp.minimum(1.0, clip_share * jnp.sqrt(jnp.float32(M * N)) / (jnp.sqrt(total) + 1e-06))

    shares = [share, second_axis(share, -1), second_axis(share, -2), second_axis(share, 1)]
    block = jnp.stack(shares, axis=1).reshape(1024, 512)
    plus = first(block, -1)
    minus = first(block, 1)
    far_a = first(plus[:512], -1)
    far_b = first(minus[512:], 1)
    sums = back_project([(0, [block])], left)
    sums = back_project([(1, [plus]), (3, [minus])], left, sums)
    u0, u1, u2, u3 = back_project([(2, [far_a, far_b])], left, sums, cut=True)
    update = ((u0 + along_x(u1, 1)) + (along_x(u3, -1) + along_x(u2, 2))) * factor
    return (update, moment_new, second_new)


def solution(mesh):
    return jax.shard_map(
        local,
        mesh=mesh,
        in_specs=(P("col", "row"), P("col", "row"), P(("row", "col"), None), P("col", "row"), P()),
        out_specs=(P("col", "row"), P("col", "row"), P(("row", "col"), None)),
        check_vma=False,
    )
```

time: 567 us -> 313 us (0.55); the launches traced: 557 us -> 311 us
  matrix products: 195 us -> 0 us
  waiting for transfers between devices: 274 us -> 115 us
  Pallas kernels: 0 us -> 118 us
  blocking collectives: 64.3 us -> 0 us
  starting transfers between devices: 0.16 us -> 57.9 us
  local copies, waits for them, and re-layouts: 2.05 us -> 16.6 us
  between operations: 14.9 us -> 1.62 us
    dot_general x4 -> x0, matrix products: 195 us -> none  [the longest x1 71.5 us: local(): jnp.einsum('ki,skw->siw', left_basis, lax.all_gather(stacked, 'row', axis...]
    reduce_scatter x2 -> x0, waiting for transfers between devices: 149 us -> none  [the longest x1 112 us: local(): lax.psum_scatter(partial_sums, 'col', scatter_dimension=1, tiled=True)]
    all_gather x2 -> x0, waiting for transfers between devices: 125 us -> none  [the longest x1 68.3 us: local(): block_rows = lax.all_gather(back, 'col', axis=0, tiled=True)]
    pallas_call x0 -> x20, Pallas kernels: none -> 118 us  [the longest x8 52.9 us: project(): call(kernel, (4,), in_specs, out_specs, out_shape, [pltpu.VMEM((rows, 102...]
    ppermute x0 -> x39, waiting for transfers between devices: none -> 115 us  [move(): return lax.ppermute(value, BOTH, pairs)]
    psum x1 -> x0, blocking collectives: 64.3 us -> none  [local(): total = lax.psum(jnp.sum(rotated * rotated), ('row', 'col'))]
    ppermute x0 -> x39, starting transfers between devices: none -> 57.9 us  [move(): return lax.ppermute(value, BOTH, pairs)]
    unnamed x9 -> x31, local copies, waits for them, and re-layouts: 2.05 us -> 15.2 us
  transfers between devices with their start and end apart: 4 -> 39, of which waited for: 4 -> 19; matrix products, arithmetic and copies ran while one was open for 0% -> 1% of each run, Pallas kernels for 0% -> 34%
where the time goes in v2:
time: 313 us; the launch traced here: 311 us
  Pallas kernels  118 us (38%)
  waiting for transfers between devices  115 us (37%)
  starting transfers between devices  57.9 us (18%)
  local copies, waits for them, and re-layouts  16.6 us (5%)
    ppermute x39, waiting for transfers between devices, move(): return lax.ppermute(value, BOTH, pairs)  115 us
    ppermute x39, starting transfers between devices, move(): return lax.ppermute(value, BOTH, pairs)  57.9 us
    pallas_call x8, Pallas kernels, project(): call(kernel, (4,), in_specs, out_specs, out_shape, [pltpu.VMEM((rows, 102...  52.9 us
    pallas_call x2, Pallas kernels, order_left(): call(kernel, (4, 4), [pl.BlockSpec((1024, 128), lambda a, b, o: (0, o[a *...  25.2 us
    pallas_call x3, Pallas kernels, back_project(): call(kernel, (4,), in_specs, out_specs, out_shape, [pltpu.VMEM((1024 * g,...  21.4 us
    unnamed x31, local copies, waits for them, and re-layouts  15.2 us
  transfers between devices with their start and end apart: 39, of which 19 were waited for; matrix products, arithmetic and copies ran while one was open for 1% of the time, Pallas kernels for 34%

profile of v2, /device:TPU:0, one launch (start us, length us, event | category | flops | bytes accessed | tf_op | source)
XLA Modules:
  0.0 311.3 jit_solution(1462764098882213810)
XLA Ops:
  5.7 9.0 %collective-permute-done = f32[128,1024]{1,0:T(8,128)S(1)} collective-permute-done((f32[128,1024]{1,0:T(8,128)S(1)}, f32[128,1024]{1,0:T(8,128)S(1)}, u32[]{:S(2)}, u32[]{:S(2)}) %collective-permute-start) | collective-permute-done | bytes 524320 | tf_op jit(solution)/shard_map/ppermute | solution.py:59
  15.4 2.8 collective-permute-start.2
  18.5 12.6 %order_left.2 = (bf16[1024,4096]{1,0:T(8,128)(2,1)S(1)}, bf16[1024,4096]{1,0:T(8,128)(2,1)}) custom-call(s32[16]{0:T(128)S(1)} %select_n.93.order_ref, f32[1024,2048]{1,0:T(8,128)} %left_ref.1), custom_call_target="tpu_custom_call" | custom-call | flops 10000000 | bytes 16777216 | tf_op jit(solution)/shard_map/order_left/pallas_call | solution.py:106
  31.1 10.3 %collective-permute-done.2.refs_1_ = f32[256,1024]{1,0:T(8,128)S(1)} collective-permute-done((f32[256,1024]{1,0:T(8,128)}, f32[256,1024]{1,0:T(8,128)S(1)}, u32[]{:S(2)}, u32[]{:S(2)}) %collective-permute-start.2) | collective-permute-done | bytes 1048608 | tf_op jit(solution)/shard_map/ppermute | solution.py:59
  41.4 3.7 %collective-permute-start.3 = (f32[128,1024]{1,0:T(8,128)S(1)}, f32[128,1024]{1,0:T(8,128)S(1)}, u32[]{:S(2)}, u32[]{:S(2)}) collective-permute-start(f32[128,1024]{1,0:T(8,128)S(1)} %slice.16), channel_id=1, source_target_pairs={{0,96},{1,97},{2,98},{3,99},{4,100},{5,101},{6,102},{7,103},{8,104... | collective-permute-start | bytes 1572872 | tf_op jit(solution)/shard_map/ppermute | solution.py:59
  45.2 12.6 %order_left.3 = (bf16[1024,4096]{1,0:T(8,128)(2,1)S(1)}, bf16[1024,4096]{1,0:T(8,128)(2,1)}) custom-call(s32[16]{0:T(128)S(1)} %select_n.93.order_ref, f32[1024,2048]{1,0:T(8,128)} %collective-permute-done.5.left_ref, bf16[1024,4096]{1,0:T(8,128)(2,1)S(1)} %get-tuple-element.36.refs_0_, ...), custom_call_target="tpu_custom_call", output_to_operand_aliasing={{0}: (2, {}), {1}: (3, {})} | custom-call | flops 10000000 | bytes 16777216 | tf_op jit(solution)/shard_map/order_left/pallas_call | solution.py:106
  57.7 7.4 %project2.3 = (f32[512,512]{1,0:T(8,128)S(1)}, f32[512,512]{1,0:T(8,128)S(1)}) custom-call(f32[256,1024]{1,0:T(8,128)} %constant_dynamic-update-slice_fusion.refs_0_, f32[256,1024]{1,0:T(8,128)S(1)} %collective-permute-done.2.refs_1_, bf16[1024,4096]{1,0:T(8,128)(2,1)S(1)} %get-tuple-element.38.refs_3_.refs_2_.refs_1_.refs_4_, ...), custom_call_target="tpu_custom_call" | custom-call | flops 3221225472 | bytes 8388608 | tf_op jit(solution)/shard_map/project2/pallas_call | solution.py:181
  65.2 3.1 collective-permute-start.15
  68.3 7.0 %project2.2 = (f32[512,512]{1,0:T(8,128)}, f32[512,512]{1,0:T(8,128)}) custom-call(f32[256,1024]{1,0:T(8,128)S(1)} %collective-permute-done.1.refs_0_, f32[128,1024]{1,0:T(8,128)S(1)} %collective-permute-done.3.refs_1_, f32[128,1024]{1,0:T(8,128)S(1)} %collective-permute-done.4.refs_2_, ...), custom_call_target="tpu_custom_call" | custom-call | flops 3221225472 | bytes 8388608 | tf_op jit(solution)/shard_map/project2/pallas_call | solution.py:181
  75.2 3.2 %collective-permute-start.8 = (f32[512,512]{1,0:T(8,128)}, f32[512,512]{1,0:T(8,128)S(1)}, u32[]{:S(2)}, u32[]{:S(2)}) collective-permute-start(f32[512,512]{1,0:T(8,128)} %get-tuple-element.41), channel_id=1, source_target_pairs={{0,12},{1,13},{2,14},{3,15},{4,0},{5,1},{6,2},{7,3},{8,4},{9,5},{1... | collective-permute-start | bytes 3145736 | tf_op jit(solution)/shard_map/ppermute | solution.py:59
  78.5 2.1 collective-permute-done.15.refs_4_
  80.6 6.3 %project3.3 = f32[512,1024]{1,0:T(8,128)S(1)} custom-call(f32[256,1024]{1,0:T(8,128)} %constant_dynamic-update-slice_fusion.refs_0_, f32[256,1024]{1,0:T(8,128)S(1)} %collective-permute-done.2.refs_1_, bf16[1024,4096]{1,0:T(8,128)(2,1)S(1)} %get-tuple-element.38.refs_3_.refs_2_.refs_1_.refs_4_, ...), custom_call_target="tpu_custom_call" | custom-call | flops 3221225472 | bytes 8388608 | tf_op jit(solution)/shard_map/project3/pallas_call | solution.py:181
  86.9 3.8 %collective-permute-start.16 = (f32[512,1024]{1,0:T(8,128)S(1)}, f32[512,1024]{1,0:T(8,128)S(1)}, u32[]{:S(2)}, u32[]{:S(2)}) collective-permute-start(f32[512,1024]{1,0:T(8,128)S(1)} %project3.3), channel_id=1, source_target_pairs={{0,12},{1,13},{2,14},{3,15},{4,0},{5,1},{6,2},{7,3},{8,4},{9,5},{1... | collective-permute-start | bytes 6291464 | tf_op jit(solution)/shard_map/ppermute | solution.py:59
  90.7 7.0 %project1.3 = f32[512,1024]{1,0:T(8,128)} custom-call(f32[256,1024]{1,0:T(8,128)} %constant_dynamic-update-slice_fusion.refs_0_, f32[256,1024]{1,0:T(8,128)S(1)} %collective-permute-done.2.refs_1_, bf16[1024,4096]{1,0:T(8,128)(2,1)S(1)} %get-tuple-element.38.refs_3_.refs_2_.refs_1_.refs_4_, ...), custom_call_target="tpu_custom_call" | custom-call | flops 3221225472 | bytes 8388608 | tf_op jit(solution)/shard_map/project1/pallas_call | solution.py:181
  97.7 6.7 %project3.2 = f32[512,1024]{1,0:T(8,128)} custom-call(f32[256,1024]{1,0:T(8,128)S(1)} %collective-permute-done.1.refs_0_, f32[128,1024]{1,0:T(8,128)S(1)} %collective-permute-done.3.refs_1_, f32[128,1024]{1,0:T(8,128)S(1)} %collective-permute-done.4.refs_2_, bf16[1024,4096]{1,0:T(8,128)(2,1)S(1)} %get-tuple-element.38.refs_3_.refs_2_.refs_1_.refs_4_, ...), custom_call_target="tpu_custom_call" | custom-call | flops 3221225472 | bytes 8388608 | tf_op jit(solution)/shard_map/project3/pallas_call | solution.py:181
  104.4 3.2 %collective-permute-start.9 = (f32[512,1024]{1,0:T(8,128)}, f32[512,1024]{1,0:T(8,128)}, u32[]{:S(2)}, u32[]{:S(2)}) collective-permute-start(f32[512,1024]{1,0:T(8,128)} %project3.2), channel_id=1, source_target_pairs={{0,12},{1,13},{2,14},{3,15},{4,0},{5,1},{6,2},{7,3},{8,4},{9,5},{1... | collective-permute-start | bytes 6291464 | tf_op jit(solution)/shard_map/ppermute | solution.py:59
  107.7 6.8 %project1.2 = f32[512,1024]{1,0:T(8,128)} custom-call(f32[256,1024]{1,0:T(8,128)S(1)} %collective-permute-done.1.refs_0_, f32[128,1024]{1,0:T(8,128)S(1)} %collective-permute-done.3.refs_1_, f32[128,1024]{1,0:T(8,128)S(1)} %collective-permute-done.4.refs_2_, bf16[1024,4096]{1,0:T(8,128)(2,1)S(1)} %get-tuple-element.38.refs_3_.refs_2_.refs_1_.refs_4_, ...), custom_call_target="tpu_custom_call" | custom-call | flops 3221225472 | bytes 8388608 | tf_op jit(solution)/shard_map/project1/pallas_call | solution.py:181
  114.4 6.0 %project0.3.a = f32[512,1024]{1,0:T(8,128)S(1)} custom-call(f32[256,1024]{1,0:T(8,128)} %constant_dynamic-update-slice_fusion.refs_0_, f32[256,1024]{1,0:T(8,128)S(1)} %collective-permute-done.2.refs_1_, bf16[1024,4096]{1,0:T(8,128)(2,1)S(1)} %get-tuple-element.38.refs_3_.refs_2_.refs_1_.refs_4_, ...), custom_call_target="tpu_custom_call" | custom-call | flops 3221225472 | bytes 8388608 | tf_op jit(solution)/shard_map/project0/pallas_call | solution.py:181
  121.9 3.3 %collective-permute-done.14.b = f32[512,1024]{1,0:T(8,128)S(1)} collective-permute-done((f32[512,1024]{1,0:T(8,128)}, f32[512,1024]{1,0:T(8,128)S(1)}, u32[]{:S(2)}, u32[]{:S(2)}) %collective-permute-start.14) | collective-permute-done | bytes 2097184 | tf_op jit(solution)/shard_map/ppermute | solution.py:59
  132.2 1.9 collective-permute-start.17
  134.1 2.1 collective-permute-start.18
  138.1 3.4 %copy-done.1 = bf16[1024,4096]{1,0:T(8,128)(2,1)S(1)} copy-done((bf16[1024,4096]{1,0:T(8,128)(2,1)S(1)}, bf16[1024,4096]{1,0:T(8,128)(2,1)}, u32[]{:S(2)}) %copy-start.1) | copy-done | bytes 8388632
  141.5 5.7 %project0.2.a = f32[512,1024]{1,0:T(8,128)S(1)} custom-call(f32[256,1024]{1,0:T(8,128)S(1)} %collective-permute-done.1.refs_0_, f32[128,1024]{1,0:T(8,128)S(1)} %collective-permute-done.3.refs_1_, f32[128,1024]{1,0:T(8,128)S(1)} %copy-done.3, bf16[1024,4096]{1,0:T(8,128)(2,1)S(1)} %copy-done.1, ...), custom_call_target="tpu_custom_call" | custom-call | flops 3221225472 | bytes 8388608 | tf_op jit(solution)/shard_map/project0/pallas_call | solution.py:181
  147.2 11.8 %collective-permute-done.7.b = f32[512,1024]{1,0:T(8,128)} collective-permute-done((f32[512,1024]{1,0:T(8,128)}, f32[512,1024]{1,0:T(8,128)}, u32[]{:S(2)}, u32[]{:S(2)}) %collective-permute-start.7) | collective-permute-done | bytes 2097184 | tf_op jit(solution)/shard_map/ppermute | solution.py:59
  159.0 4.2 %settle.2 = (f32[512,256]{1,0:T(8,128)S(1)}, f32[512,256]{1,0:T(8,128)}, f32[512,256]{1,0:T(8,128)}, f32[512,256]{1,0:T(8,128)}) custom-call(f32[512,1024]{1,0:T(8,128)S(1)} %project0.2.a, f32[512,1024]{1,0:T(8,128)} %collective-permute-done.7.b, f32[512,1024]{1,0:T(8,128)} %collective-permute-done.9.c), custom_call_target="tpu_custom_call" | custom-call | flops 1048576 | bytes 8388608 | tf_op jit(solution)/shard_map/settle/pallas_call | solution.py:197
  165.1 2.2 collective-permute-start.11
  167.3 4.7 %collective-permute-start.12 = (f32[512,256]{1,0:T(8,128)}, f32[512,256]{1,0:T(8,128)S(1)}, u32[]{:S(2)}, u32[]{:S(2)}) collective-permute-start(f32[512,256]{1,0:T(8,128)} %get-tuple-element.45), channel_id=1, source_target_pairs={{0,2},{1,3},{2,0},{3,1},{4,6},{5,7},{6,4},{7,5},{8,10},{9,11},{10,... | collective-permute-start | bytes 1572872 | tf_op jit(solution)/shard_map/ppermute | solution.py:59
  172.1 2.2 copy-done.4
  175.7 3.6 %rotate.2.refs_6_ = f32[256,1024]{1,0:T(8,128)S(1)} custom-call(f32[512,256]{1,0:T(8,128)S(1)} %get-tuple-element.50.refs_0_, f32[512,256]{1,0:T(8,128)} %collective-permute-done.17.refs_1_, f32[512,256]{1,0:T(8,128)} %collective-permute-done.18.refs_2_, f32[512,256]{1,0:T(8,128)} %collective-permute-done.19.refs_3_, ...), custom_call_target="tpu_custom_call" | custom-call | flops 805306368 | bytes 8388608 | tf_op jit(solution)/shard_map/rotate/pallas_call | solution.py:232
  179.3 3.5 %collective-permute-done.12.refs_3_ = f32[512,256]{1,0:T(8,128)S(1)} collective-permute-done((f32[512,256]{1,0:T(8,128)}, f32[512,256]{1,0:T(8,128)S(1)}, u32[]{:S(2)}, u32[]{:S(2)}) %collective-permute-start.12) | collective-permute-done | bytes 524320 | tf_op jit(solution)/shard_map/ppermute | solution.py:59
  182.9 2.5 rotate.3
  187.3 3.9 %turn.1 = (f32[128,1024]{1,0:T(8,128)}, f32[128,512]{1,0:T(8,128)S(1)}, f32[128,512]{1,0:T(8,128)S(1)}, f32[8,128]{1,0:T(8,128)S(1)}) custom-call(s32[1]{0:T(128)} %bitcast.core_ref, f32[128,1024]{1,0:T(8,128)S(1)} %get-tuple-element.54.own_ref, f32[128,1024]{1,0:T(8,128)S(1)} %collective-permute-done.20.other_ref, f32[128,1024]{1,0:T(8,128)S(1)} %copy-done.9, ...), custom_call_target="tpu_custom_call" | custom-call | flops 805306368 | bytes 7340032 | tf_op jit(solution)/shard_map/turn/pallas_call | solution.py:273
  192.9 2.7 collective-permute-start.22
  197.0 10.9 %collective-permute-done.22 = f32[2,128,512]{2,1,0:T(8,128)S(1)} collective-permute-done((f32[2,128,512]{2,1,0:T(8,128)S(1)}, f32[2,128,512]{2,1,0:T(8,128)S(1)}, u32[]{:S(2)}, u32[]{:S(2)}) %collective-permute-start.22) | collective-permute-done | bytes 524320 | tf_op jit(solution)/shard_map/ppermute | solution.py:59
  207.9 3.9 %collective-permute-done.24 = f32[2,128,512]{2,1,0:T(8,128)S(1)} collective-permute-done((f32[2,128,512]{2,1,0:T(8,128)S(1)}, f32[2,128,512]{2,1,0:T(8,128)S(1)}, u32[]{:S(2)}, u32[]{:S(2)}) %collective-permute-start.24) | collective-permute-done | bytes 524320 | tf_op jit(solution)/shard_map/ppermute | solution.py:59
  212.3 2.0 collective-permute-start.27
  214.3 24.0 %collective-permute-done.25.refs_0_ = f32[1024,512]{1,0:T(8,128)S(1)} collective-permute-done((f32[1024,512]{1,0:T(8,128)S(1)}, f32[1024,512]{1,0:T(8,128)S(1)}, u32[]{:S(2)}, u32[]{:S(2)}) %collective-permute-start.25) | collective-permute-done | bytes 2097184 | tf_op jit(solution)/shard_map/ppermute | solution.py:59
  240.9 5.5 %back_project.3.refs_6_ = f32[1024,512]{1,0:T(8,128)S(1)} custom-call(f32[1024,512]{1,0:T(8,128)S(1)} %bitcast.13, bf16[1024,4096]{1,0:T(8,128)(2,1)S(1)} %bitcast.10, bf16[1024,4096]{1,0:T(8,128)(2,1)} %get-tuple-element.39.refs_4_.refs_3_.refs_2_.refs_5_), custom_call_target="tpu_custom_call" | custom-call | flops 3221225472 | bytes 10485760 | tf_op jit(solution)/shard_map/back_project/pallas_call | solution.py:328
  246.3 9.4 %back_project.4.refs_4_ = f32[1024,512]{1,0:T(8,128)S(1)} custom-call(f32[1024,512]{1,0:T(8,128)S(1)} %collective-permute-done.25.refs_0_, f32[1024,512]{1,0:T(8,128)S(1)} %collective-permute-done.27.refs_1_, bf16[1024,4096]{1,0:T(8,128)(2,1)} %copy-done, bf16[1024,4096]{1,0:T(8,128)(2,1)} %get-tuple-element.39.refs_4_.refs_3_.refs_2_.refs_5_, ...), custom_call_target="tpu_custom_call" | custom-call | flops 6442450944 | bytes 16777216 | tf_op jit(solution)/shard_map/back_project/pallas_call | solution.py:328
  256.1 6.5 %back_project.5 = (f32[1024,128]{1,0:T(8,128)S(1)}, f32[1024,128]{1,0:T(8,128)}, f32[1024,128]{1,0:T(8,128)S(1)}, f32[1024,128]{1,0:T(8,128)S(1)}) custom-call(f32[512,512]{1,0:T(8,128)S(1)} %collective-permute-done.26.refs_0_, f32[512,512]{1,0:T(8,128)S(1)} %collective-permute-done.28.refs_1_, bf16[1024,4096]{1,0:T(8,128)(2,1)} %copy-done, ...), custom_call_target="tpu_custom_call" | custom-call | flops 3221225472 | bytes 10485760 | tf_op jit(solution)/shard_map/back_project/pallas_call | solution.py:328
  262.6 3.7 %collective-permute-start.30 = (f32[1024,128]{1,0:T(8,128)S(1)}, f32[1024,128]{1,0:T(8,128)S(1)}, u32[]{:S(2)}, u32[]{:S(2)}) collective-permute-start(f32[1024,128]{1,0:T(8,128)S(1)} %get-tuple-element.60), channel_id=1, source_target_pairs={{0,96},{1,97},{2,98},{3,99},{4,100},{5,101},{6,102},{7,103},{8,104... | collective-permute-start | bytes 1572872 | tf_op jit(solution)/shard_map/ppermute | solution.py:59
  270.4 14.7 %collective-permute-done.33 = f32[8,128]{1,0:T(8,128)S(1)} collective-permute-done((f32[8,128]{1,0:T(8,128)S(1)}, f32[8,128]{1,0:T(8,128)S(1)}, u32[]{:S(2)}, u32[]{:S(2)}) %collective-permute-start.33) | collective-permute-done | bytes 4128 | tf_op jit(solution)/shard_map/ppermute | solution.py:59
  285.1 5.0 %collective-permute-start.34 = (f32[8,128]{1,0:T(8,128)S(1)}, f32[8,128]{1,0:T(8,128)S(1)}, u32[]{:S(2)}, u32[]{:S(2)}) collective-permute-start(f32[8,128]{1,0:T(8,128)S(1)} %add.215), channel_id=1, source_target_pairs={{0,64},{1,65},{2,66},{3,67},{4,68},{5,69},{6,70},{7,71},{8,72},{9,... | collective-permute-start | bytes 12296 | tf_op jit(solution)/shard_map/ppermute | solution.py:59
  291.7 3.6 %collective-permute-done.35 = f32[8,128]{1,0:T(8,128)S(1)} collective-permute-done((f32[8,128]{1,0:T(8,128)S(1)}, f32[8,128]{1,0:T(8,128)S(1)}, u32[]{:S(2)}, u32[]{:S(2)}) %collective-permute-start.35) | collective-permute-done | bytes 4128 | tf_op jit(solution)/shard_map/ppermute | solution.py:59
  295.5 4.9 %collective-permute-done.36 = f32[8,128]{1,0:T(8,128)S(1)} collective-permute-done((f32[8,128]{1,0:T(8,128)S(1)}, f32[8,128]{1,0:T(8,128)S(1)}, u32[]{:S(2)}, u32[]{:S(2)}) %collective-permute-start.36) | collective-permute-done | bytes 4128 | tf_op jit(solution)/shard_map/ppermute | solution.py:59
  300.4 3.6 %collective-permute-done.37 = f32[8,128]{1,0:T(8,128)S(1)} collective-permute-done((f32[8,128]{1,0:T(8,128)S(1)}, f32[8,128]{1,0:T(8,128)S(1)}, u32[]{:S(2)}, u32[]{:S(2)}) %collective-permute-start.37) | collective-permute-done | bytes 4128 | tf_op jit(solution)/shard_map/ppermute | solution.py:59
  304.0 2.2 collective-permute-start.38
  306.2 2.9 collective-permute-done.38
  (106 shorter events, 35.7 us)
Async XLA Ops:
  0.6 44.5 %collective-permute-start.5 = (f32[1024,2048]{1,0:T(8,128)}, f32[1024,2048]{1,0:T(8,128)}, u32[]{:S(2)}, u32[]{:S(2)}) collective-permute-start(f32[1024,2048]{1,0:T(8,128)} %left_ref.1), channel_id=1, source_target_pairs={{0,16},{1,17},{2,18},{3,19},{4,20},{5,21},{6,22},{7,23},{8,24},{9,... | collective-permute-start | bytes 25165832 | tf_op jit(solution)/shard_map/ppermute | solution.py:59
  4.4 10.3 %collective-permute-start = (f32[128,1024]{1,0:T(8,128)S(1)}, f32[128,1024]{1,0:T(8,128)S(1)}, u32[]{:S(2)}, u32[]{:S(2)}) collective-permute-start(f32[128,1024]{1,0:T(8,128)S(1)} %get-tuple-element.35), channel_id=1, source_target_pairs={{0,16},{1,17},{2,18},{3,19},{4,20},{5,21},{6,22},{7,23},{8,24},{9,... | collective-permute-start | bytes 1572872 | tf_op jit(solution)/shard_map/ppermute | solution.py:59
  15.4 25.9 %collective-permute-start.2 = (f32[256,1024]{1,0:T(8,128)}, f32[256,1024]{1,0:T(8,128)S(1)}, u32[]{:S(2)}, u32[]{:S(2)}) collective-permute-start(f32[256,1024]{1,0:T(8,128)} %constant_dynamic-update-slice_fusion.refs_0_), channel_id=1, source_target_pairs={{0,96},{1,97},{2,98},{3,99},{4,100},{5,101},{6,102},{7,103},{8,104... | collective-permute-start | bytes 3145736 | tf_op jit(solution)/shard_map/ppermute | solution.py:59
  18.3 26.7 %collective-permute-start.1 = (f32[256,1024]{1,0:T(8,128)}, f32[256,1024]{1,0:T(8,128)S(1)}, u32[]{:S(2)}, u32[]{:S(2)}) collective-permute-start(f32[256,1024]{1,0:T(8,128)} %constant_dynamic-update-slice_fusion.refs_0_), channel_id=1, source_target_pairs={{0,32},{1,33},{2,34},{3,35},{4,36},{5,37},{6,38},{7,39},{8,40},{9,... | collective-permute-start | bytes 3145736 | tf_op jit(solution)/shard_map/ppermute | solution.py:59
  41.4 26.9 %collective-permute-start.3 = (f32[128,1024]{1,0:T(8,128)S(1)}, f32[128,1024]{1,0:T(8,128)S(1)}, u32[]{:S(2)}, u32[]{:S(2)}) collective-permute-start(f32[128,1024]{1,0:T(8,128)S(1)} %slice.16), channel_id=1, source_target_pairs={{0,96},{1,97},{2,98},{3,99},{4,100},{5,101},{6,102},{7,103},{8,104... | collective-permute-start | bytes 1572872 | tf_op jit(solution)/shard_map/ppermute | solution.py:59
  45.1 23.2 %collective-permute-start.4 = (f32[128,1024]{1,0:T(8,128)S(1)}, f32[128,1024]{1,0:T(8,128)S(1)}, u32[]{:S(2)}, u32[]{:S(2)}) collective-permute-start(f32[128,1024]{1,0:T(8,128)S(1)} %slice.17), channel_id=1, source_target_pairs={{0,32},{1,33},{2,34},{3,35},{4,36},{5,37},{6,38},{7,39},{8,40},{9,... | collective-permute-start | bytes 1572872 | tf_op jit(solution)/shard_map/ppermute | solution.py:59
  57.7 56.7 %copy-start = (bf16[1024,4096]{1,0:T(8,128)(2,1)}, bf16[1024,4096]{1,0:T(8,128)(2,1)S(1)}, u32[]{:S(2)}) copy-start(bf16[1024,4096]{1,0:T(8,128)(2,1)S(1)} %get-tuple-element.38.refs_3_.refs_2_.refs_1_.refs_4_) | copy-start | bytes 25165828
  65.2 15.4 %collective-permute-start.15 = (f32[512,512]{1,0:T(8,128)S(1)}, f32[512,512]{1,0:T(8,128)S(1)}, u32[]{:S(2)}, u32[]{:S(2)}) collective-permute-start(f32[512,512]{1,0:T(8,128)S(1)} %get-tuple-element.49), channel_id=1, source_target_pairs={{0,12},{1,13},{2,14},{3,15},{4,0},{5,1},{6,2},{7,3},{8,4},{9,5},{1... | collective-permute-start | bytes 3145736 | tf_op jit(solution)/shard_map/ppermute | solution.py:59
  68.3 22.4 %collective-permute-start.13 = (f32[512,512]{1,0:T(8,128)S(1)}, f32[512,512]{1,0:T(8,128)S(1)}, u32[]{:S(2)}, u32[]{:S(2)}) collective-permute-start(f32[512,512]{1,0:T(8,128)S(1)} %get-tuple-element.48), channel_id=1, source_target_pairs={{0,4},{1,5},{2,6},{3,7},{4,8},{5,9},{6,10},{7,11},{8,12},{9,13},{1... | collective-permute-start | bytes 3145736 | tf_op jit(solution)/shard_map/ppermute | solution.py:59
  68.3 39.4 %copy-start.2 = (f32[128,1024]{1,0:T(8,128)}, f32[128,1024]{1,0:T(8,128)S(1)}, u32[]{:S(2)}) copy-start(f32[128,1024]{1,0:T(8,128)S(1)} %collective-permute-done.4.refs_2_) | copy-start | bytes 1572868
  75.2 22.5 %collective-permute-start.8 = (f32[512,512]{1,0:T(8,128)}, f32[512,512]{1,0:T(8,128)S(1)}, u32[]{:S(2)}, u32[]{:S(2)}) collective-permute-start(f32[512,512]{1,0:T(8,128)} %get-tuple-element.41), channel_id=1, source_target_pairs={{0,12},{1,13},{2,14},{3,15},{4,0},{5,1},{6,2},{7,3},{8,4},{9,5},{1... | collective-permute-start | bytes 3145736 | tf_op jit(solution)/shard_map/ppermute | solution.py:59
  78.5 29.2 %collective-permute-start.6 = (f32[512,512]{1,0:T(8,128)}, f32[512,512]{1,0:T(8,128)S(1)}, u32[]{:S(2)}, u32[]{:S(2)}) collective-permute-start(f32[512,512]{1,0:T(8,128)} %get-tuple-element.40), channel_id=1, source_target_pairs={{0,4},{1,5},{2,6},{3,7},{4,8},{5,9},{6,10},{7,11},{8,12},{9,13},{1... | collective-permute-start | bytes 3145736 | tf_op jit(solution)/shard_map/ppermute | solution.py:59
  86.9 33.5 %collective-permute-start.16 = (f32[512,1024]{1,0:T(8,128)S(1)}, f32[512,1024]{1,0:T(8,128)S(1)}, u32[]{:S(2)}, u32[]{:S(2)}) collective-permute-start(f32[512,1024]{1,0:T(8,128)S(1)} %project3.3), channel_id=1, source_target_pairs={{0,12},{1,13},{2,14},{3,15},{4,0},{5,1},{6,2},{7,3},{8,4},{9,5},{1... | collective-permute-start | bytes 6291464 | tf_op jit(solution)/shard_map/ppermute | solution.py:59
  97.7 27.5 %collective-permute-start.14 = (f32[512,1024]{1,0:T(8,128)}, f32[512,1024]{1,0:T(8,128)S(1)}, u32[]{:S(2)}, u32[]{:S(2)}) collective-permute-start(f32[512,1024]{1,0:T(8,128)} %project1.3), channel_id=1, source_target_pairs={{0,4},{1,5},{2,6},{3,7},{4,8},{5,9},{6,10},{7,11},{8,12},{9,13},{1... | collective-permute-start | bytes 6291464 | tf_op jit(solution)/shard_map/ppermute | solution.py:59
  104.4 42.8 %collective-permute-start.9 = (f32[512,1024]{1,0:T(8,128)}, f32[512,1024]{1,0:T(8,128)}, u32[]{:S(2)}, u32[]{:S(2)}) collective-permute-start(f32[512,1024]{1,0:T(8,128)} %project3.2), channel_id=1, source_target_pairs={{0,12},{1,13},{2,14},{3,15},{4,0},{5,1},{6,2},{7,3},{8,4},{9,5},{1... | collective-permute-start | bytes 6291464 | tf_op jit(solution)/shard_map/ppermute | solution.py:59
  114.4 44.6 %collective-permute-start.7 = (f32[512,1024]{1,0:T(8,128)}, f32[512,1024]{1,0:T(8,128)}, u32[]{:S(2)}, u32[]{:S(2)}) collective-permute-start(f32[512,1024]{1,0:T(8,128)} %project1.2), channel_id=1, source_target_pairs={{0,4},{1,5},{2,6},{3,7},{4,8},{5,9},{6,10},{7,11},{8,12},{9,13},{1... | collective-permute-start | bytes 6291464 | tf_op jit(solution)/shard_map/ppermute | solution.py:59
  120.4 17.7 %copy-start.3 = (f32[128,1024]{1,0:T(8,128)S(1)}, f32[128,1024]{1,0:T(8,128)}, u32[]{:S(2)}) copy-start(f32[128,1024]{1,0:T(8,128)} %copy-done.2) | copy-start | bytes 1572868
  126.5 1.6 copy-start.6
  132.2 35.0 %collective-permute-start.17 = (f32[512,256]{1,0:T(8,128)}, f32[512,256]{1,0:T(8,128)}, u32[]{:S(2)}, u32[]{:S(2)}) collective-permute-start(f32[512,256]{1,0:T(8,128)} %get-tuple-element.51), channel_id=1, source_target_pairs={{0,1},{1,2},{2,3},{3,0},{4,5},{5,6},{6,7},{7,4},{8,9},{9,10},{10,1... | collective-permute-start | bytes 1572872 | tf_op jit(solution)/shard_map/ppermute | solution.py:59
  134.1 41.6 %collective-permute-start.18 = (f32[512,256]{1,0:T(8,128)}, f32[512,256]{1,0:T(8,128)}, u32[]{:S(2)}, u32[]{:S(2)}) collective-permute-start(f32[512,256]{1,0:T(8,128)} %copy-done.12), channel_id=1, source_target_pairs={{0,3},{1,0},{2,1},{3,2},{4,7},{5,4},{6,5},{7,6},{8,11},{9,8},{10,9... | collective-permute-start | bytes 1572872 | tf_op jit(solution)/shard_map/ppermute | solution.py:59
  136.3 39.5 %collective-permute-start.19 = (f32[512,256]{1,0:T(8,128)S(1)}, f32[512,256]{1,0:T(8,128)}, u32[]{:S(2)}, u32[]{:S(2)}) collective-permute-start(f32[512,256]{1,0:T(8,128)S(1)} %get-tuple-element.53), channel_id=1, source_target_pairs={{0,2},{1,3},{2,0},{3,1},{4,6},{5,7},{6,4},{7,5},{8,10},{9,11},{10,... | collective-permute-start | bytes 1572872 | tf_op jit(solution)/shard_map/ppermute | solution.py:59
  138.1 3.4 %copy-start.1 = (bf16[1024,4096]{1,0:T(8,128)(2,1)S(1)}, bf16[1024,4096]{1,0:T(8,128)(2,1)}, u32[]{:S(2)}) copy-start(bf16[1024,4096]{1,0:T(8,128)(2,1)} %copy-done) | copy-start | bytes 25165828
  163.2 16.2 %collective-permute-start.10 = (f32[512,256]{1,0:T(8,128)}, f32[512,256]{1,0:T(8,128)S(1)}, u32[]{:S(2)}, u32[]{:S(2)}) collective-permute-start(f32[512,256]{1,0:T(8,128)} %get-tuple-element.43), channel_id=1, source_target_pairs={{0,1},{1,2},{2,3},{3,0},{4,5},{5,6},{6,7},{7,4},{8,9},{9,10},{10,1... | collective-permute-start | bytes 1572872 | tf_op jit(solution)/shard_map/ppermute | solution.py:59
  165.1 14.2 %collective-permute-start.11 = (f32[512,256]{1,0:T(8,128)}, f32[512,256]{1,0:T(8,128)S(1)}, u32[]{:S(2)}, u32[]{:S(2)}) collective-permute-start(f32[512,256]{1,0:T(8,128)} %get-tuple-element.44), channel_id=1, source_target_pairs={{0,3},{1,0},{2,1},{3,2},{4,7},{5,4},{6,5},{7,6},{8,11},{9,8},{10,9... | collective-permute-start | bytes 1572872 | tf_op jit(solution)/shard_map/ppermute | solution.py:59
  167.3 15.6 %collective-permute-start.12 = (f32[512,256]{1,0:T(8,128)}, f32[512,256]{1,0:T(8,128)S(1)}, u32[]{:S(2)}, u32[]{:S(2)}) collective-permute-start(f32[512,256]{1,0:T(8,128)} %get-tuple-element.45), channel_id=1, source_target_pairs={{0,2},{1,3},{2,0},{3,1},{4,6},{5,7},{6,4},{7,5},{8,10},{9,11},{10,... | collective-permute-start | bytes 1572872 | tf_op jit(solution)/shard_map/ppermute | solution.py:59
  172.1 2.2 copy-start.4
  182.9 4.5 %copy-start.9 = (f32[128,1024]{1,0:T(8,128)S(1)}, f32[128,1024]{1,0:T(8,128)}, u32[]{:S(2)}) copy-start(f32[128,1024]{1,0:T(8,128)} %second_ref.1) | copy-start | bytes 1572868
  185.3 2.0 collective-permute-start.20
  187.3 53.5 %slice-start = ((s8[8388608]{0:T(1024)(128)(4,1)}), s8[4194304]{0:T(1024)(128)(4,1)S(1)}, s32[]{:S(2)}) async-start(s8[8388608]{0:T(1024)(128)(4,1)} %bitcast.9), calls=%async_computation | async-start | bytes 8388608
  191.3 1.5 collective-permute-start.21
  192.9 15.0 %collective-permute-start.22 = (f32[2,128,512]{2,1,0:T(8,128)S(1)}, f32[2,128,512]{2,1,0:T(8,128)S(1)}, u32[]{:S(2)}, u32[]{:S(2)}) collective-permute-start(f32[2,128,512]{2,1,0:T(8,128)S(1)} %get-tuple-element.66), channel_id=1, source_target_pairs={{0,3},{1,0},{2,1},{3,2},{4,7},{5,4},{6,5},{7,6},{8,11},{9,8},{10,9... | collective-permute-start | bytes 1572872 | tf_op jit(solution)/shard_map/ppermute | solution.py:59
  195.6 12.4 %collective-permute-start.23 = (f32[2,128,512]{2,1,0:T(8,128)S(1)}, f32[2,128,512]{2,1,0:T(8,128)S(1)}, u32[]{:S(2)}, u32[]{:S(2)}) collective-permute-start(f32[2,128,512]{2,1,0:T(8,128)S(1)} %get-tuple-element.66), channel_id=1, source_target_pairs={{0,2},{1,3},{2,0},{3,1},{4,6},{5,7},{6,4},{7,5},{8,10},{9,11},{10,... | collective-permute-start | bytes 1572872 | tf_op jit(solution)/shard_map/ppermute | solution.py:59
  197.0 14.9 %collective-permute-start.24 = (f32[2,128,512]{2,1,0:T(8,128)S(1)}, f32[2,128,512]{2,1,0:T(8,128)S(1)}, u32[]{:S(2)}, u32[]{:S(2)}) collective-permute-start(f32[2,128,512]{2,1,0:T(8,128)S(1)} %get-tuple-element.66), channel_id=1, source_target_pairs={{0,1},{1,2},{2,3},{3,0},{4,5},{5,6},{6,7},{7,4},{8,9},{9,10},{10,1... | collective-permute-start | bytes 1572872 | tf_op jit(solution)/shard_map/ppermute | solution.py:59
  211.9 29.0 %slice-start.1 = ((s8[8388608]{0:T(1024)(128)(4,1)}), s8[4194304]{0:T(1024)(128)(4,1)S(1)}, s32[]{:S(2)}) async-start(s8[8388608]{0:T(1024)(128)(4,1)} %bitcast.9), calls=%async_computation.1 | async-start | bytes 8388608
  212.2 26.1 %collective-permute-start.25 = (f32[1024,512]{1,0:T(8,128)S(1)}, f32[1024,512]{1,0:T(8,128)S(1)}, u32[]{:S(2)}, u32[]{:S(2)}) collective-permute-start(f32[1024,512]{1,0:T(8,128)S(1)} %bitcast.11), channel_id=1, source_target_pairs={{0,12},{1,13},{2,14},{3,15},{4,0},{5,1},{6,2},{7,3},{8,4},{9,5},{1... | collective-permute-start | bytes 6291464 | tf_op jit(solution)/shard_map/ppermute | solution.py:59
  212.3 27.4 %collective-permute-start.27 = (f32[1024,512]{1,0:T(8,128)S(1)}, f32[1024,512]{1,0:T(8,128)S(1)}, u32[]{:S(2)}, u32[]{:S(2)}) collective-permute-start(f32[1024,512]{1,0:T(8,128)S(1)} %bitcast.12), channel_id=1, source_target_pairs={{0,4},{1,5},{2,6},{3,7},{4,8},{5,9},{6,10},{7,11},{8,12},{9,13},{1... | collective-permute-start | bytes 6291464 | tf_op jit(solution)/shard_map/ppermute | solution.py:59
  238.4 17.4 %collective-permute-start.26 = (f32[512,512]{1,0:T(8,128)S(1)}, f32[512,512]{1,0:T(8,128)S(1)}, u32[]{:S(2)}, u32[]{:S(2)}) collective-permute-start(f32[512,512]{1,0:T(8,128)S(1)} %slice.18), channel_id=1, source_target_pairs={{0,12},{1,13},{2,14},{3,15},{4,0},{5,1},{6,2},{7,3},{8,4},{9,5},{1... | collective-permute-start | bytes 3145736 | tf_op jit(solution)/shard_map/ppermute | solution.py:59
  239.8 16.3 %collective-permute-start.28 = (f32[512,512]{1,0:T(8,128)S(1)}, f32[512,512]{1,0:T(8,128)S(1)}, u32[]{:S(2)}, u32[]{:S(2)}) collective-permute-start(f32[512,512]{1,0:T(8,128)S(1)} %slice.19), channel_id=1, source_target_pairs={{0,4},{1,5},{2,6},{3,7},{4,8},{5,9},{6,10},{7,11},{8,12},{9,13},{1... | collective-permute-start | bytes 3145736 | tf_op jit(solution)/shard_map/ppermute | solution.py:59
  262.5 47.8 %collective-permute-start.29 = (f32[1024,128]{1,0:T(8,128)}, f32[1024,128]{1,0:T(8,128)S(1)}, u32[]{:S(2)}, u32[]{:S(2)}) collective-permute-start(f32[1024,128]{1,0:T(8,128)} %get-tuple-element.59), channel_id=1, source_target_pairs={{0,32},{1,33},{2,34},{3,35},{4,36},{5,37},{6,38},{7,39},{8,40},{9,... | collective-permute-start | bytes 1572872 | tf_op jit(solution)/shard_map/ppermute | solution.py:59
  262.6 47.7 %collective-permute-start.30 = (f32[1024,128]{1,0:T(8,128)S(1)}, f32[1024,128]{1,0:T(8,128)S(1)}, u32[]{:S(2)}, u32[]{:S(2)}) collective-permute-start(f32[1024,128]{1,0:T(8,128)S(1)} %get-tuple-element.60), channel_id=1, source_target_pairs={{0,96},{1,97},{2,98},{3,99},{4,100},{5,101},{6,102},{7,103},{8,104... | collective-permute-start | bytes 1572872 | tf_op jit(solution)/shard_map/ppermute | solution.py:59
  266.3 44.1 %collective-permute-start.31 = (f32[1024,128]{1,0:T(8,128)S(1)}, f32[1024,128]{1,0:T(8,128)S(1)}, u32[]{:S(2)}, u32[]{:S(2)}) collective-permute-start(f32[1024,128]{1,0:T(8,128)S(1)} %get-tuple-element.61), channel_id=1, source_target_pairs={{0,64},{1,65},{2,66},{3,67},{4,68},{5,69},{6,70},{7,71},{8,72},{9,... | collective-permute-start | bytes 1572872 | tf_op jit(solution)/shard_map/ppermute | solution.py:59
  267.8 1.2 collective-permute-start.32
  268.9 16.2 %collective-permute-start.33 = (f32[8,128]{1,0:T(8,128)S(1)}, f32[8,128]{1,0:T(8,128)S(1)}, u32[]{:S(2)}, u32[]{:S(2)}) collective-permute-start(f32[8,128]{1,0:T(8,128)S(1)} %add.214), channel_id=1, source_target_pairs={{0,32},{1,33},{2,34},{3,35},{4,36},{5,37},{6,38},{7,39},{8,40},{9,... | collective-permute-start | bytes 12296 | tf_op jit(solution)/shard_map/ppermute | solution.py:59
  285.1 6.5 %collective-permute-start.34 = (f32[8,128]{1,0:T(8,128)S(1)}, f32[8,128]{1,0:T(8,128)S(1)}, u32[]{:S(2)}, u32[]{:S(2)}) collective-permute-start(f32[8,128]{1,0:T(8,128)S(1)} %add.215), channel_id=1, source_target_pairs={{0,64},{1,65},{2,66},{3,67},{4,68},{5,69},{6,70},{7,71},{8,72},{9,... | collective-permute-start | bytes 12296 | tf_op jit(solution)/shard_map/ppermute | solution.py:59
  291.6 3.6 %collective-permute-start.35 = (f32[8,128]{1,0:T(8,128)S(1)}, f32[8,128]{1,0:T(8,128)S(1)}, u32[]{:S(2)}, u32[]{:S(2)}) collective-permute-start(f32[8,128]{1,0:T(8,128)S(1)} %add.216), channel_id=1, source_target_pairs={{0,4},{1,5},{2,6},{3,7},{4,0},{5,1},{6,2},{7,3},{8,12},{9,13},{10,... | collective-permute-start | bytes 12296 | tf_op jit(solution)/shard_map/ppermute | solution.py:59
  295.3 5.1 %collective-permute-start.36 = (f32[8,128]{1,0:T(8,128)S(1)}, f32[8,128]{1,0:T(8,128)S(1)}, u32[]{:S(2)}, u32[]{:S(2)}) collective-permute-start(f32[8,128]{1,0:T(8,128)S(1)} %add.217), channel_id=1, source_target_pairs={{0,8},{1,9},{2,10},{3,11},{4,12},{5,13},{6,14},{7,15},{8,0},{9,1},... | collective-permute-start | bytes 12296 | tf_op jit(solution)/shard_map/ppermute | solution.py:59
  300.4 3.6 %collective-permute-start.37 = (f32[8,128]{1,0:T(8,128)S(1)}, f32[8,128]{1,0:T(8,128)S(1)}, u32[]{:S(2)}, u32[]{:S(2)}) collective-permute-start(f32[8,128]{1,0:T(8,128)S(1)} %add.218), channel_id=1, source_target_pairs={{0,1},{1,0},{2,3},{3,2},{4,5},{5,4},{6,7},{7,6},{8,9},{9,8},{10,11... | collective-permute-start | bytes 12296 | tf_op jit(solution)/shard_map/ppermute | solution.py:59
  304.0 5.1 %collective-permute-start.38 = (f32[8,128]{1,0:T(8,128)S(1)}, f32[8,128]{1,0:T(8,128)S(1)}, u32[]{:S(2)}, u32[]{:S(2)}) collective-permute-start(f32[8,128]{1,0:T(8,128)S(1)} %add.219), channel_id=1, source_target_pairs={{0,2},{1,3},{2,0},{3,1},{4,6},{5,7},{6,4},{7,5},{8,10},{9,11},{10,... | collective-permute-start | bytes 12296 | tf_op jit(solution)/shard_map/ppermute | solution.py:59
  (6 other events, 7.2 us)

commit v3 on v2

v3 whole, which is shorter than its diff:
```python
import functools

import jax
import jax.numpy as jnp
import numpy as np
from jax import lax
from jax.experimental import pallas as pl
from jax.experimental.pallas import tpu as pltpu
from jax.sharding import PartitionSpec as P

M = 16384
N = 1024

first_decay = 0.9
second_decay = 0.95
epsilon = 1e-08
clip_share = 0.25

f32, bf16 = jnp.float32, jnp.bfloat16
BOTH = ("row", "col")
VMEM_LIMIT = 50 * 1024 * 1024
SHRINK = 64
CHIPS = (1, 3, 2, 0)


def call(kernel, grid, in_specs, out_specs, out_shape, scratch=(), flops=0, moved=0, aliases=None, prefetch=0, name=None, after=()):
    at, k = prefetch + len(in_specs), len(after)

    def body(*refs):
        kernel(*refs[:at], *refs[at + k :])

    run = pl.pallas_call(
        body,
        grid_spec=pltpu.PrefetchScalarGridSpec(
            num_scalar_prefetch=prefetch, grid=grid, in_specs=list(in_specs) + [pl.BlockSpec(memory_space=pl.ANY)] * k,
            out_specs=out_specs, scratch_shapes=list(scratch),
        ),
        out_shape=out_shape,
        input_output_aliases=aliases or {},
        compiler_params=pltpu.CompilerParams(vmem_limit_bytes=VMEM_LIMIT, dimension_semantics=("arbitrary",) * len(grid)),
        cost_estimate=pl.CostEstimate(flops=flops // SHRINK, bytes_accessed=moved // SHRINK, transcendentals=0),
        name=name,
    )
    return lambda *args: run(*args, *after)


def shape(rows, columns, dtype=f32):
    return jax.ShapeDtypeStruct((rows, columns), dtype)


def split(value):
    high = value.astype(bf16)
    return high, (value - high.astype(f32)).astype(bf16)


def dot3(a_high, a_low, b_high, b_low, dims=(((1,), (0,)), ((), ()))):
    d = functools.partial(lax.dot_general, dimension_numbers=dims, preferred_element_type=f32)
    return d(a_high, b_high) + (d(a_high, b_low) + d(a_low, b_high))


def move(value, step):
    pairs = []
    for x in range(4):
        for c in range(2):
            for y in range(4):
                for z in range(4):
                    tx, tc, ty, tz = step(x, c, y, z)
                    pairs.append(((2 * x + c) * 16 + 4 * y + z, (2 * (tx % 4) + tc) * 16 + 4 * (ty % 4) + tz % 4))
    return lax.ppermute(value, BOTH, pairs)


def swap(value):
    return move(value, lambda x, c, y, z: (x, 1 - c, y, z))


def along_x(value, d):
    return move(value, lambda x, c, y, z: (x + d, c, y, z))


def first(value, d):
    return move(value, lambda x, c, y, z: (x, c, y + d, z) if c == 0 else (x, c, y, z + d))


def second_axis(value, d):
    return move(value, lambda x, c, y, z: (x, c, y, z + d) if c == 0 else (x, c, y + d, z))


def start(core, grad, moment):
    def kernel(core_ref, grad_ref, moment_ref, new_ref, keep_ref, give_ref):
        g = grad_ref[...]
        new = first_decay * moment_ref[...] + (1.0 - first_decay) * g
        new_ref[...] = new
        g, new = g.T, new.T
        zero = core_ref[0] == 0
        keep_ref[...] = jnp.where(zero, g, new)
        give_ref[...] = jnp.where(zero, new, g)

    block = pl.BlockSpec((256, 128), lambda t, c: (t, 0))
    turned = pl.BlockSpec((128, 256), lambda t, c: (0, t))
    return call(
        kernel, (4,), [block, block], [block, turned, turned], [shape(1024, 128), shape(128, 1024), shape(128, 1024)],
        moved=3 * 2**20, flops=10**6, prefetch=1, name="start",
    )(core, grad, moment)


def order_left(order, left, half, held=None):
    def kernel(order_ref, left_ref, *refs):
        high_ref, low_ref = refs[-2:]
        for a in range(4):
            for b in range(4):
                at = pl.multiple_of(order_ref[a * 4 + b] * 128, 128)
                high, low = split(left_ref[:, pl.ds(at, 128)])
                high_ref[a, 0, :, b * 128 : b * 128 + 128] = high
                low_ref[a, 0, :, b * 128 : b * 128 + 128] = low

    out = pl.BlockSpec((4, 1, 128, 512), lambda t, o: (0, half, t, 0))
    anywhere = pl.BlockSpec(memory_space=pl.ANY)
    more = [] if held is None else list(held)
    return call(
        kernel, (8,), [pl.BlockSpec((128, 2048), lambda t, o: (t, 0))] + [anywhere] * len(more),
        [out, out], [jax.ShapeDtypeStruct((4, 2, 1024, 512), bf16)] * 2, moved=16 * 2**20, flops=10**7,
        aliases={2: 0, 3: 1} if more else None, prefetch=1, name="order_left",
    )(order, left, *more)


def order_right(order, right):
    def kernel(order_ref, right_ref, high_ref, low_ref):
        high, low = split(right_ref[...])
        high_ref[...] = high
        low_ref[...] = low

    out = pl.BlockSpec((128, 1024), lambda a, o: (a, 0))
    return call(
        kernel, (8,), [pl.BlockSpec((128, 1024), lambda a, o: (o[a], 0))], [out, out], [shape(1024, 1024, bf16)] * 2,
        moved=8 * 2**20, flops=10**6, prefetch=1, name="order_right",
    )(order, right)


def fill(refs, high, low):
    at = 0
    for ref in refs:
        size = ref.shape[0]
        high[at : at + size, :], low[at : at + size, :] = split(ref[...])
        at += size


def project_far(blocks, left, after=()):
    rows = sum(b.shape[0] for b in blocks)
    n = len(blocks)

    def kernel(*refs):
        lh, ll, one, two, gh, gl = refs[n:]
        t = pl.program_id(0)

        @pl.when(t == 0)
        def _():
            fill(refs[:n], gh, gl)

        value = dot3(gh[...], gl[...], lh[0, 0], ll[0, 0])

        @pl.when(t == 0)
        def _():
            one[...] = value

        @pl.when(t == 1)
        def _():
            two[...] = value

    column = pl.BlockSpec((1, 1, 1024, 512), lambda t: (2, t, 0, 0))
    whole = pl.BlockSpec((rows, 512), lambda t: (0, 0))
    return call(
        kernel, (2,), [pl.BlockSpec(b.shape, lambda t: (0, 0)) for b in blocks] + [column, column],
        [whole, whole], [shape(rows, 512)] * 2, [pltpu.VMEM((rows, 1024), bf16)] * 2,
        flops=6 * rows * 2**20, moved=4 * 2**20 + rows * 8192, name="project_far", after=after,
    )(*blocks, *left)


def project_near(blocks, left, near, far, after=()):
    rows = sum(b.shape[0] for b in blocks)
    n = len(blocks)

    def kernel(*refs):
        lh, ll, near_ref, far_ref, up, down, gh, gl = refs[n:]
        t = pl.program_id(0)

        @pl.when(t == 0)
        def _():
            fill(refs[:n], gh, gl)

        value = dot3(gh[...], gl[...], lh[0, 0], ll[0, 0])

        @pl.when(t == 0)
        def _():
            up[...] = value + near_ref[...]

        @pl.when(t == 1)
        def _():
            up[...] = value

        @pl.when(t == 2)
        def _():
            down[...] = value

        @pl.when(t == 3)
        def _():
            down[...] = value + far_ref[...]

    column = pl.BlockSpec((1, 1, 1024, 512), lambda t: (t // 2 * 2 + 1, t % 2, 0, 0))
    whole = pl.BlockSpec((rows, 512), lambda t: (0, 0))
    return call(
        kernel, (4,), [pl.BlockSpec(b.shape, lambda t: (0, 0)) for b in blocks] + [column, column, whole, whole],
        [pl.BlockSpec((rows, 512), lambda t: (0, jnp.minimum(t, 1))), pl.BlockSpec((rows, 512), lambda t: (0, jnp.maximum(t - 2, 0)))],
        [shape(rows, 1024)] * 2, [pltpu.VMEM((rows, 1024), bf16)] * 2,
        flops=12 * rows * 2**20, moved=8 * 2**20 + rows * 16384, name="project_near", after=after,
    )(*blocks, *left, near, far)


def project_own(blocks, left, up, down, after=()):
    rows = sum(b.shape[0] for b in blocks)
    n = len(blocks)

    def kernel(*refs):
        lh, ll, up0, up1, down0, down1 = refs[n : n + 6]
        outs, (gh, gl) = refs[n + 6 : n + 10], refs[n + 10 :]
        t = pl.program_id(0)

        @pl.when(t == 0)
        def _():
            fill(refs[:n], gh, gl)

        high = jnp.concatenate([lh[0, 0], lh[0, 1]], axis=1)
        low = jnp.concatenate([ll[0, 0], ll[0, 1]], axis=1)
        value = dot3(gh[...], gl[...], high, low)
        value = value + jnp.concatenate([up0[...] + down0[...], up1[...] + down1[...]], axis=1)
        for d in range(4):

            @pl.when(t == d)
            def _(d=d):
                outs[d][...] = value

    column = pl.BlockSpec((1, 2, 1024, 128), lambda t: (0, 0, 0, t))
    one, two = pl.BlockSpec((rows, 128), lambda t: (0, t)), pl.BlockSpec((rows, 128), lambda t: (0, 4 + t))
    whole = pl.BlockSpec((rows, 256), lambda t: (0, 0))
    return call(
        kernel, (4,), [pl.BlockSpec(b.shape, lambda t: (0, 0)) for b in blocks] + [column, column, one, two, one, two],
        [whole] * 4, [shape(rows, 256)] * 4, [pltpu.VMEM((rows, 1024), bf16)] * 2,
        flops=6 * rows * 2**20, moved=4 * 2**20 + rows * 16384, name="project_own", after=after,
    )(*blocks, *left, up, up, down, down)


def rotate(parts, right, chips, before=None, last=False):
    rows = parts[0].shape[0]
    n = 6 + (before is not None)

    def kernel(*refs):
        p, (rh, rl) = refs[:4], refs[4:6]
        th, tl = refs[-2:]
        t = pl.program_id(0)

        @pl.when(t == 0)
        def _():
            total = (p[0][...] + p[1][...]) + (p[2][...] + p[3][...])
            th[...], tl[...] = split(total.T)

        def pick(r):
            places = [h * 512 + CHIPS.index(d) * 128 for d in chips for h in range(2)]
            return jnp.concatenate([r[p : p + 128, :] for p in places], axis=0)

        value = dot3(th[...], tl[...], pick(rh), pick(rl))
        if before is not None:
            value = value + refs[6][...]
        if last:
            refs[n][...] = value[:128]
            refs[n + 1][...] = value[128:]
        else:
            refs[n][...] = value

    part = pl.BlockSpec((rows, 256), lambda t: (0, 0))
    column = pl.BlockSpec((1024, 256), lambda t: (0, t))
    tall = pl.BlockSpec((256, 256), lambda t: (0, t))
    flat = pl.BlockSpec((128, 256), lambda t: (0, t))
    return call(
        kernel, (4,), [part] * 4 + [column] * 2 + [tall] * (n - 6),
        [flat, flat] if last else tall, [shape(128, 1024)] * 2 if last else shape(256, 1024),
        [pltpu.VMEM((256, rows), bf16)] * 2, flops=6 * 256 * rows * 1024, moved=8 * 2**20, name="rotate",
    )(*parts, *right, *([before] if n > 6 else []))


def turn(core, own, other, second, right):
    def kernel(core_ref, own_ref, other_ref, second_ref, rh, rl, new_ref, keep_ref, give_ref, th, tl, sum_ref):
        t = pl.program_id(0)

        @pl.when(t == 0)
        def _():
            zero = core_ref[0] == 0
            a, b = own_ref[...], other_ref[...]
            g, m = jnp.where(zero, a, b), jnp.where(zero, b, a)
            new = second_decay * second_ref[...] + (1.0 - second_decay) * g * g
            new_ref[...] = new
            rotated = m / (jnp.sqrt(new) + epsilon)
            th[...], tl[...] = split(rotated)
            squares = rotated * rotated
            total = squares[0:8, :]
            for i in range(1, 16):
                total = total + squares[i * 8 : i * 8 + 8, :]
            narrow = total[:, 0:128]
            for i in range(1, 8):
                narrow = narrow + total[:, i * 128 : i * 128 + 128]
            sum_ref[...] = narrow

        value = dot3(th[...], tl[...], rh[...], rl[...], (((1,), (1,)), ((), ())))
        first_lanes = jnp.where(t % 2 == 0, sum_ref[...], 0.0)
        extra = jnp.concatenate([first_lanes, jnp.zeros((8, 128), f32)], axis=1)

        @pl.when(t < 2)
        def _():
            keep_ref[0:128, :] = value
            keep_ref[128:136, :] = extra

        @pl.when(t >= 2)
        def _():
            give_ref[0:128, :] = value
            give_ref[128:136, :] = extra

    whole = pl.BlockSpec((128, 1024), lambda t, c: (0, 0))
    rows = pl.BlockSpec((256, 1024), lambda t, c: (t, 0))
    return call(
        kernel, (4,), [whole, whole, whole, rows, rows],
        [
            whole,
            pl.BlockSpec((136, 256), lambda t, c: (0, jnp.minimum(t, 1))),
            pl.BlockSpec((136, 256), lambda t, c: (0, jnp.maximum(t - 2, 0))),
        ],
        [shape(128, 1024), shape(136, 512), shape(136, 512)],
        [pltpu.VMEM((128, 1024), bf16)] * 2 + [pltpu.VMEM((8, 128), f32)],
        flops=6 * 128 * 2**20, moved=7 * 2**20, prefetch=1, name="turn",
    )(core, own, other, second, *right)


def back_project(terms, left, before=None, cut=False, after=()):
    arrays = [a for _, group in terms for a, _ in group]
    sizes = [size for _, group in terms for _, size in group]
    n, g = len(arrays), len(terms)

    def kernel(*refs):
        s_refs, l_refs = refs[:n], refs[n : n + 2 * g]
        sh, sl = refs[-2:]
        outs = refs[n + 2 * g + (before is not None) : -2]
        t = pl.program_id(0)

        @pl.when(t == 0)
        def _():
            fill(s_refs, sh, sl)

        value = refs[n + 2 * g][...] if before is not None else None
        for i in range(g):
            rows = slice(i * 1024, i * 1024 + 1024)
            high, low = l_refs[2 * i], l_refs[2 * i + 1]
            high = jnp.concatenate([high[0, 0], high[0, 1]], axis=1)
            low = jnp.concatenate([low[0, 0], low[0, 1]], axis=1)
            new = dot3(high, low, sh[rows, :], sl[rows, :])
            value = new if value is None else value + new
        if cut:
            outs[0][...] = value[:, :128]
            outs[1][...] = value[:, 128:]
        else:
            outs[0][...] = value

    wide = pl.BlockSpec((256, 256), lambda t: (t, 0))
    in_specs = [pl.BlockSpec((size, 256), lambda t: (0, 0)) for size in sizes]
    args = list(arrays)
    for d, _ in terms:
        in_specs += [pl.BlockSpec((1, 2, 256, 512), lambda t, d=d: (d, 0, t, 0))] * 2
        args += list(left)
    if before is not None:
        in_specs.append(wide)
        args.append(before)
    if cut:
        out_specs, out_shape = [pl.BlockSpec((256, 128), lambda t: (t, 0))] * 2, [shape(1024, 128)] * 2
    else:
        out_specs, out_shape = wide, shape(1024, 256)
    return call(
        kernel, (4,), in_specs, out_specs, out_shape, [pltpu.VMEM((1024 * g, 256), bf16)] * 2,
        flops=3 * g * 2**29, moved=(5 * g + 2) * 2**20, name="back_project", after=after,
    )(*args)


def lay(shares, half, after=()):
    def kernel(*refs):
        out = refs[-1]
        extra = jnp.zeros((8, 256), f32)
        for d in range(4):
            for h in range(2):
                out[(h * 4 + d) * 128 : (h * 4 + d) * 128 + 128, :] = refs[d][h, 0:128, :]
                extra = extra + refs[d][h, 128:136, :]
        out[1024:1032, :] = extra

    part = pl.BlockSpec((2, 136, 256), lambda t: (0, 0, half))
    return call(
        kernel, (1,), [part] * 4, pl.BlockSpec((1032, 256), lambda t: (0, 0)), shape(1032, 256),
        flops=2**14, moved=2**21, name="lay", after=after,
    )(*shares)


def tables():
    left = np.zeros((2, 16, 16), np.int32)
    right = np.zeros((8, 8), np.int32)
    for c in range(2):
        for y in range(4):
            for z in range(4):
                for a in range(4):
                    for b in range(4):
                        p, q = (y + a, z + b) if c == 0 else (y + b, z + a)
                        left[c, y * 4 + z, a * 4 + b] = p % 4 * 4 + q % 4
        for x in range(4):
            for h in range(2):
                for i, d in enumerate(CHIPS):
                    right[2 * x + c, h * 4 + i] = 2 * ((x + d) % 4) + (c + h) % 2
    return left, right


def local(grad, moment, second, left_basis, right_basis):
    row, col = lax.axis_index("row"), lax.axis_index("col")
    core = (row % 2).reshape(1).astype(jnp.int32)
    by_col, by_row = tables()
    order = jnp.asarray(by_col)[row % 2, col]
    order_r = jnp.asarray(by_row)[row]

    left_other = swap(left_basis)
    moment_new, keep, give = start(core, grad, moment)
    moved = swap(give)
    left = order_left(order, left_basis, 0)
    right = order_right(order_r, right_basis)
    mine = jnp.concatenate([keep, moved], axis=0)
    plus = along_x(mine, -1)
    minus = along_x(mine, 1)
    left = order_left(order, left_other, 1, left)
    far_a = along_x(plus[:128], -1)
    far_b = along_x(minus[128:], 1)

    chunks = [((0,), [mine]), ((1, 3), [plus, minus]), ((2,), [far_a, far_b])]
    far, near, parts = [None] * 3, [None] * 3, [None] * 3

    def step_far(i, after=()):
        one, two = project_far(chunks[i][1], left, after)
        far[i] = first(one, 1), first(two, -1)
        return (one,)

    def step_near(i, after=()):
        up, down = project_near(chunks[i][1], left, *far[i], after)
        near[i] = first(up, 1), first(down, -1)
        return (up,)

    def step_own(i, after=()):
        q = project_own(chunks[i][1], left, *near[i], after)
        parts[i] = [q[0], second_axis(q[1], 1), second_axis(q[3], -1), second_axis(q[2], 2)]
        return (q[0],)

    done = step_far(0)
    done = step_near(0, done)
    done = step_far(1, done)
    done = step_own(0, done)
    done = step_far(2, done)
    done = step_near(1, done)
    done = step_near(2, done)
    done = step_own(1, done)
    done = step_own(2, done)
    part = None
    for i, (chips, _) in enumerate(chunks):
        part = rotate(parts[i], right, chips, part, last=i == 2)
    own, other = part
    other = swap(other)

    second_new, keep, give = turn(core, own, other, second, right)
    share = jnp.stack([keep, swap(give)], axis=0)
    shares = [share, second_axis(share, -1), second_axis(share, -2), second_axis(share, 1)]

    block_a = lay(shares, 0)
    plus_a, minus_a = first(block_a, -1), first(block_a, 1)
    sums = back_project([(0, [(block_a, 1024)])], left)
    far_a, far_b = first(plus_a[:512], -1), first(minus_a[512:], 1)
    block_b = lay(shares, 1, (plus_a, minus_a))
    plus_b, minus_b = first(block_b, -1), first(block_b, 1)
    sums = back_project([(1, [(plus_a, 1024)]), (3, [(minus_a, 1024)])], left, sums, after=(block_b,))
    u1, u3 = back_project([(2, [(far_a, 512), (far_b, 512)])], left, sums, cut=True)
    got1, got3 = along_x(u1, 1), along_x(u3, -1)
    squares = (block_a[1024:, :128] + plus_a[1024:, :128]) + (minus_a[1024:, :128] + far_b[512:, :128])
    squares = squares + move(squares, lambda x, c, y, z: (x ^ 1, c, y, z))
    squares = squares + move(squares, lambda x, c, y, z: (x ^ 2, c, y, z))
    sums = back_project([(0, [(block_b, 1024)])], left, after=(u1,))
    far_a, far_b = first(plus_b[:512], -1), first(minus_b[512:1024], 1)
    sums = back_project([(1, [(plus_b, 1024)]), (3, [(minus_b, 1024)])], left, sums)
    u2, u0 = back_project([(2, [(far_a, 512), (far_b, 512)])], left, sums, cut=True, after=(squares,))
    total = jnp.sum(squares)
    factor = jnp.minimum(1.0, clip_share * jnp.sqrt(jnp.float32(M * N)) / (jnp.sqrt(total) + 1e-06))
    update = ((u0 + got1) + (got3 + along_x(u2, 2))) * factor
    return (update, moment_new, second_new)


def solution(mesh):
    return jax.shard_map(
        local,
        mesh=mesh,
        in_specs=(P("col", "row"), P("col", "row"), P(("row", "col"), None), P("col", "row"), P()),
        out_specs=(P("col", "row"), P("col", "row"), P(("row", "col"), None)),
        check_vma=False,
    )
```

time: 313 us -> 325 us (1.038)
  Pallas kernels: 118 us -> 135 us
  waiting for transfers between devices: 115 us -> 107 us
    pallas_call x20 -> x25, Pallas kernels: 118 us -> 135 us  [call(): return lambda *args: run(*args, *after)]
    ppermute x39 -> x45, waiting for transfers between devices: 115 us -> 107 us  [move(): return lax.ppermute(value, BOTH, pairs)]
    unnamed x31 -> x49, local copies, waits for them, and re-layouts: 15.2 us -> 11.7 us
    ppermute x39 -> x45, starting transfers between devices: 57.9 us -> 59.2 us  [move(): return lax.ppermute(value, BOTH, pairs)]
  transfers between devices with their start and end apart: 39 -> 45, of which waited for: 19 -> 18; matrix products, arithmetic and copies ran while one was open for 1% -> 2% of each run, Pallas kernels for 34% -> 31%
where the time goes in v3:
time: 325 us; the launch traced here: 323 us
  Pallas kernels  135 us (42%)
  waiting for transfers between devices  107 us (33%)
  starting transfers between devices  59.2 us (18%)
  local copies, waits for them, and re-layouts  16.5 us (5%)
  other arithmetic  3.26 us (1%)
    pallas_call x25, Pallas kernels, call(): return lambda *args: run(*args, *after)  135 us
    ppermute x45, waiting for transfers between devices, move(): return lax.ppermute(value, BOTH, pairs)  107 us
    ppermute x45, starting transfers between devices, move(): return lax.ppermute(value, BOTH, pairs)  59.2 us
    unnamed x49, local copies, waits for them, and re-layouts  11.7 us
  transfers between devices with their start and end apart: 45, of which 18 were waited for; matrix products, arithmetic and copies ran while one was open for 2% of the time, Pallas kernels for 31%

profile of v3, /device:TPU:0, one launch (start us, length us, event | category | flops | bytes accessed | tf_op | source)
XLA Modules:
  0.0 323.1 jit_solution(4777023594054624469)
XLA Ops:
  5.5 9.9 %order_left.2 = (bf16[4,2,1024,512]{3,2,1,0:T(8,128)(2,1)}, bf16[4,2,1024,512]{3,2,1,0:T(8,128)(2,1)}) custom-call(s32[16]{0:T(128)S(1)} %dynamic-slice_bitcast_fusion.1.refs_0_, f32[1024,2048]{1,0:T(8,128)} %refs_1_.4), custom_call_target="tpu_custom_call" | custom-call | flops 156250 | bytes 262144 | tf_op jit(solution)/shard_map/order_left/pallas_call | solution.py:44
  15.5 9.9 %order_left.3 = (bf16[4,2,1024,512]{3,2,1,0:T(8,128)(2,1)}, bf16[4,2,1024,512]{3,2,1,0:T(8,128)(2,1)}) custom-call(s32[16]{0:T(128)S(1)} %dynamic-slice_bitcast_fusion.1.refs_0_, f32[1024,2048]{1,0:T(8,128)} %collective-permute-done.5.refs_1_, bf16[4,2,1024,512]{3,2,1,0:T(8,128)(2,1)} %get-tuple-element.47.refs_2_, ...), custom_call_target="tpu_custom_call", output_to_operand_aliasing={{0}: (2, {}), {1}: (3, {})} | custom-call | flops 156250 | bytes 262144 | tf_op jit(solution)/shard_map/order_left/pallas_call | solution.py:44
  25.4 3.7 %project_far.3 = (f32[256,512]{1,0:T(8,128)S(1)}, f32[256,512]{1,0:T(8,128)S(1)}) custom-call(f32[256,1024]{1,0:T(8,128)S(1)} %constant_dynamic-update-slice_fusion.refs_0_, bf16[4,2,1024,512]{3,2,1,0:T(8,128)(2,1)} %get-tuple-element.49.refs_1_.refs_2_.refs_4_, bf16[4,2,1024,512]{3,2,1,0:T(8,128)(2,1)} %get-tuple-element.50.refs_2_.refs_3_.refs_5_), custom_call_target="tpu_custom_call" | custom-call | flops 25165824 | bytes 98304 | tf_op jit(solution)/shard_map/project_far/pallas_call | solution.py:44
  32.4 2.8 collective-permute-start.1
  35.3 4.3 %collective-permute-done.6.refs_3_ = f32[256,512]{1,0:T(8,128)S(1)} collective-permute-done((f32[256,512]{1,0:T(8,128)S(1)}, f32[256,512]{1,0:T(8,128)S(1)}, u32[]{:S(2)}, u32[]{:S(2)}) %collective-permute-start.6) | collective-permute-done | bytes 524320 | tf_op jit(solution)/shard_map/ppermute | solution.py:69
  40.0 7.0 %project_near.3 = (f32[256,1024]{1,0:T(8,128)S(1)}, f32[256,1024]{1,0:T(8,128)S(1)}) custom-call(f32[256,1024]{1,0:T(8,128)} %copy-done.3, bf16[4,2,1024,512]{3,2,1,0:T(8,128)(2,1)} %get-tuple-element.49.refs_1_.refs_2_.refs_4_, bf16[4,2,1024,512]{3,2,1,0:T(8,128)(2,1)} %get-tuple-element.50.refs_2_.refs_3_.refs_5_, ...), custom_call_target="tpu_custom_call" | custom-call | flops 50331648 | bytes 196608 | tf_op jit(solution)/shard_map/project_near/pallas_call | solution.py:44
  50.3 8.1 %collective-permute-done.1.refs_0_ = f32[256,1024]{1,0:T(8,128)S(1)} collective-permute-done((f32[256,1024]{1,0:T(8,128)S(1)}, f32[256,1024]{1,0:T(8,128)S(1)}, u32[]{:S(2)}, u32[]{:S(2)}) %collective-permute-start.1) | collective-permute-done | bytes 1048608 | tf_op jit(solution)/shard_map/ppermute | solution.py:69
  58.5 3.4 %collective-permute-done.3.refs_1_ = f32[256,1024]{1,0:T(8,128)S(1)} collective-permute-done((f32[256,1024]{1,0:T(8,128)S(1)}, f32[256,1024]{1,0:T(8,128)S(1)}, u32[]{:S(2)}, u32[]{:S(2)}) %collective-permute-start.3) | collective-permute-done | bytes 1048608 | tf_op jit(solution)/shard_map/ppermute | solution.py:69
  62.9 5.9 %project_far.4 = (f32[512,512]{1,0:T(8,128)S(1)}, f32[512,512]{1,0:T(8,128)S(1)}) custom-call(f32[256,1024]{1,0:T(8,128)S(1)} %collective-permute-done.1.refs_0_, f32[256,1024]{1,0:T(8,128)} %copy-done.1, bf16[4,2,1024,512]{3,2,1,0:T(8,128)(2,1)} %get-tuple-element.49.refs_1_.refs_2_.refs_4_, ...), custom_call_target="tpu_custom_call" | custom-call | flops 50331648 | bytes 131072 | tf_op jit(solution)/shard_map/project_far/pallas_call | solution.py:44
  69.4 2.8 collective-permute-start.13
  76.5 4.8 %project_own.3 = (f32[256,256]{1,0:T(8,128)S(1)}, f32[256,256]{1,0:T(8,128)S(1)}, f32[256,256]{1,0:T(8,128)S(1)}, f32[256,256]{1,0:T(8,128)S(1)}) custom-call(f32[256,1024]{1,0:T(8,128)S(1)} %copy-done.4, bf16[4,2,1024,512]{3,2,1,0:T(8,128)(2,1)} %get-tuple-element.49.refs_1_.refs_2_.refs_4_, ...), custom_call_target="tpu_custom_call" | custom-call | flops 25165824 | bytes 131072 | tf_op jit(solution)/shard_map/project_own/pallas_call | solution.py:44
  81.3 3.8 %collective-permute-done.2.refs_0_ = f32[128,1024]{1,0:T(8,128)S(1)} collective-permute-done((f32[128,1024]{1,0:T(8,128)S(1)}, f32[128,1024]{1,0:T(8,128)S(1)}, u32[]{:S(2)}, u32[]{:S(2)}) %collective-permute-start.2) | collective-permute-done | bytes 524320 | tf_op jit(solution)/shard_map/ppermute | solution.py:69
  85.1 2.6 collective-permute-done.4.refs_1_
  87.7 3.9 %project_far.5 = (f32[256,512]{1,0:T(8,128)S(1)}, f32[256,512]{1,0:T(8,128)S(1)}) custom-call(f32[128,1024]{1,0:T(8,128)S(1)} %collective-permute-done.2.refs_0_, f32[128,1024]{1,0:T(8,128)S(1)} %collective-permute-done.4.refs_1_, bf16[4,2,1024,512]{3,2,1,0:T(8,128)(2,1)} %get-tuple-element.49.refs_1_.refs_2_.refs_4_, ...), custom_call_target="tpu_custom_call" | custom-call | flops 25165824 | bytes 98304 | tf_op jit(solution)/shard_map/project_far/pallas_call | solution.py:44
  92.6 11.2 %project_near.4 = (f32[512,1024]{1,0:T(8,128)}, f32[512,1024]{1,0:T(8,128)}) custom-call(f32[256,1024]{1,0:T(8,128)S(1)} %collective-permute-done.1.refs_0_, f32[256,1024]{1,0:T(8,128)S(1)} %copy-done.2, bf16[4,2,1024,512]{3,2,1,0:T(8,128)(2,1)} %get-tuple-element.49.refs_1_.refs_2_.refs_4_, ...), custom_call_target="tpu_custom_call" | custom-call | flops 100663296 | bytes 262144 | tf_op jit(solution)/shard_map/project_near/pallas_call | solution.py:44
  104.8 2.2 collective-permute-start.17
  107.1 3.2 %collective-permute-start.11 = (f32[256,512]{1,0:T(8,128)S(1)}, f32[256,512]{1,0:T(8,128)S(1)}, u32[]{:S(2)}, u32[]{:S(2)}) collective-permute-start(f32[256,512]{1,0:T(8,128)S(1)} %get-tuple-element.58), channel_id=1, source_target_pairs={{0,12},{1,13},{2,14},{3,15},{4,0},{5,1},{6,2},{7,3},{8,4},{9,5},{1... | collective-permute-start | bytes 1572872 | tf_op jit(solution)/shard_map/ppermute | solution.py:69
  110.3 26.6 %collective-permute-done.10.refs_4_ = f32[256,512]{1,0:T(8,128)S(1)} collective-permute-done((f32[256,512]{1,0:T(8,128)S(1)}, f32[256,512]{1,0:T(8,128)S(1)}, u32[]{:S(2)}, u32[]{:S(2)}) %collective-permute-start.10) | collective-permute-done | bytes 524320 | tf_op jit(solution)/shard_map/ppermute | solution.py:69
  136.9 7.5 %project_near.5 = (f32[256,1024]{1,0:T(8,128)S(1)}, f32[256,1024]{1,0:T(8,128)}) custom-call(f32[128,1024]{1,0:T(8,128)S(1)} %collective-permute-done.2.refs_0_, f32[128,1024]{1,0:T(8,128)S(1)} %collective-permute-done.4.refs_1_, bf16[4,2,1024,512]{3,2,1,0:T(8,128)(2,1)} %get-tuple-element.49.refs_1_.refs_2_.refs_4_, ...), custom_call_target="tpu_custom_call" | custom-call | flops 50331648 | bytes 196608 | tf_op jit(solution)/shard_map/project_near/pallas_call | solution.py:44
  149.1 8.3 %project_own.4 = (f32[512,256]{1,0:T(8,128)S(1)}, f32[512,256]{1,0:T(8,128)S(1)}, f32[512,256]{1,0:T(8,128)}, f32[512,256]{1,0:T(8,128)}) custom-call(f32[256,1024]{1,0:T(8,128)S(1)} %collective-permute-done.1.refs_0_, f32[256,1024]{1,0:T(8,128)} %copy-done.1, bf16[4,2,1024,512]{3,2,1,0:T(8,128)(2,1)} %get-tuple-element.49.refs_1_.refs_2_.refs_4_, ...), custom_call_target="tpu_custom_call" | custom-call | flops 50331648 | bytes 196608 | tf_op jit(solution)/shard_map/project_own/pallas_call | solution.py:44
  157.3 3.3 %collective-permute-start.22 = (f32[512,256]{1,0:T(8,128)}, f32[512,256]{1,0:T(8,128)S(1)}, u32[]{:S(2)}, u32[]{:S(2)}) collective-permute-start(f32[512,256]{1,0:T(8,128)} %get-tuple-element.72), channel_id=1, source_target_pairs={{0,3},{1,0},{2,1},{3,2},{4,7},{5,4},{6,5},{7,6},{8,11},{9,8},{10,9... | collective-permute-start | bytes 1572872 | tf_op jit(solution)/shard_map/ppermute | solution.py:69
  162.0 4.1 %collective-permute-done.14.refs_4_.refs_5_ = f32[256,1024]{1,0:T(8,128)S(1)} collective-permute-done((f32[256,1024]{1,0:T(8,128)S(1)}, f32[256,1024]{1,0:T(8,128)S(1)}, u32[]{:S(2)}, u32[]{:S(2)}) %collective-permute-start.14) | collective-permute-done | bytes 1048608 | tf_op jit(solution)/shard_map/ppermute | solution.py:69
  167.4 5.7 %project_own.5 = (f32[256,256]{1,0:T(8,128)S(1)}, f32[256,256]{1,0:T(8,128)}, f32[256,256]{1,0:T(8,128)}, f32[256,256]{1,0:T(8,128)}) custom-call(f32[128,1024]{1,0:T(8,128)S(1)} %collective-permute-done.2.refs_0_, f32[128,1024]{1,0:T(8,128)S(1)} %collective-permute-done.4.refs_1_, bf16[4,2,1024,512]{3,2,1,0:T(8,128)(2,1)} %get-tuple-element.49.refs_1_.refs_2_.refs_4_, ...), custom_call_target="tpu_custom_call" | custom-call | flops 25165824 | bytes 131072 | tf_op jit(solution)/shard_map/project_own/pallas_call | solution.py:44
  173.1 5.6 %collective-permute-done.25.refs_2_ = f32[256,256]{1,0:T(8,128)S(1)} collective-permute-done((f32[256,256]{1,0:T(8,128)S(1)}, f32[256,256]{1,0:T(8,128)S(1)}, u32[]{:S(2)}, u32[]{:S(2)}) %collective-permute-start.25) | collective-permute-done | bytes 262176 | tf_op jit(solution)/shard_map/ppermute | solution.py:69
  179.5 3.7 %collective-permute-start.19 = (f32[256,256]{1,0:T(8,128)}, f32[256,256]{1,0:T(8,128)}, u32[]{:S(2)}, u32[]{:S(2)}) collective-permute-start(f32[256,256]{1,0:T(8,128)} %get-tuple-element.67), channel_id=1, source_target_pairs={{0,3},{1,0},{2,1},{3,2},{4,7},{5,4},{6,5},{7,6},{8,11},{9,8},{10,9... | collective-permute-start | bytes 786440 | tf_op jit(solution)/shard_map/ppermute | solution.py:69
  185.6 6.8 %order_right.1 = (bf16[1024,1024]{1,0:T(8,128)(2,1)S(1)}, bf16[1024,1024]{1,0:T(8,128)(2,1)}) custom-call(s32[8]{0:T(128)S(1)} %dynamic-slice_bitcast_fusion.refs_0_, f32[1024,1024]{1,0:T(8,128)} %refs_1_.5), custom_call_target="tpu_custom_call" | custom-call | flops 15625 | bytes 131072 | tf_op jit(solution)/shard_map/order_right/pallas_call | solution.py:44
  193.7 3.6 %rotate.3.refs_6_ = f32[256,1024]{1,0:T(8,128)S(1)} custom-call(f32[256,256]{1,0:T(8,128)S(1)} %get-tuple-element.56.refs_4_.refs_0_, f32[256,256]{1,0:T(8,128)S(1)} %collective-permute-done.24.refs_1_, f32[256,256]{1,0:T(8,128)S(1)} %collective-permute-done.25.refs_2_, f32[256,256]{1,0:T(8,128)S(1)} %copy-done.17, bf16[1024,1024]{1,0:T(8,128)(2,1)} %copy-done, ...), custom_call_target="tpu_custom_call" | custom-call | flops 6291456 | bytes 131072 | tf_op jit(solution)/shard_map/rotate/pallas_call | solution.py:44
  198.3 4.1 %rotate.4.refs_6_ = f32[256,1024]{1,0:T(8,128)S(1)} custom-call(f32[512,256]{1,0:T(8,128)S(1)} %get-tuple-element.64.refs_8_.refs_0_, f32[512,256]{1,0:T(8,128)S(1)} %collective-permute-done.21.refs_1_, f32[512,256]{1,0:T(8,128)S(1)} %collective-permute-done.22.refs_2_, f32[512,256]{1,0:T(8,128)S(1)} %collective-permute-done.23.refs_3_, ...), custom_call_target="tpu_custom_call" | custom-call | flops 12582912 | bytes 131072 | tf_op jit(solution)/shard_map/rotate/pallas_call | solution.py:44
  202.4 3.8 %rotate.5 = (f32[128,1024]{1,0:T(8,128)S(1)}, f32[128,1024]{1,0:T(8,128)S(1)}) custom-call(f32[256,256]{1,0:T(8,128)S(1)} %get-tuple-element.65.refs_0_, f32[256,256]{1,0:T(8,128)S(1)} %collective-permute-done.18.refs_1_, f32[256,256]{1,0:T(8,128)} %collective-permute-done.19.refs_2_, f32[256,256]{1,0:T(8,128)} %collective-permute-done.20.refs_3_, ...), custom_call_target="tpu_custom_call" | custom-call | flops 6291456 | bytes 131072 | tf_op jit(solution)/shard_map/rotate/pallas_call | solution.py:44
  208.2 5.7 %turn.1 = (f32[128,1024]{1,0:T(8,128)}, f32[136,512]{1,0:T(8,128)S(1)}, f32[136,512]{1,0:T(8,128)S(1)}) custom-call(s32[1]{0:T(128)} %bitcast.refs_0_, f32[128,1024]{1,0:T(8,128)S(1)} %get-tuple-element.77.refs_1_, f32[128,1024]{1,0:T(8,128)S(1)} %collective-permute-done.27.refs_2_, f32[128,1024]{1,0:T(8,128)S(1)} %copy-done.13, bf16[1024,1024]{1,0:T(8,128)(2,1)} %copy-done, ...), custom_call_target="tpu_custom_call" | custom-call | flops 12582912 | bytes 114688 | tf_op jit(solution)/shard_map/turn/pallas_call | solution.py:44
  216.2 2.7 collective-permute-start.30
  218.9 6.3 %collective-permute-done.29.refs_1_ = f32[2,136,512]{2,1,0:T(8,128)S(1)} collective-permute-done((f32[2,136,512]{2,1,0:T(8,128)S(1)}, f32[2,136,512]{2,1,0:T(8,128)S(1)}, u32[]{:S(2)}, u32[]{:S(2)}) %collective-permute-start.29) | collective-permute-done | bytes 557088 | tf_op jit(solution)/shard_map/ppermute | solution.py:69
  225.1 2.2 collective-permute-done.30.refs_2_
  227.3 5.9 %collective-permute-done.31.refs_3_ = f32[2,136,512]{2,1,0:T(8,128)S(1)} collective-permute-done((f32[2,136,512]{2,1,0:T(8,128)S(1)}, f32[2,136,512]{2,1,0:T(8,128)S(1)}, u32[]{:S(2)}, u32[]{:S(2)}) %collective-permute-start.31) | collective-permute-done | bytes 557088 | tf_op jit(solution)/shard_map/ppermute | solution.py:69
  233.4 3.1 collective-permute-start.32
  236.6 12.9 %collective-permute-done.33.refs_5_.refs_1_ = f32[1032,256]{1,0:T(8,128)S(1)} collective-permute-done((f32[1032,256]{1,0:T(8,128)S(1)}, f32[1032,256]{1,0:T(8,128)S(1)}, u32[]{:S(2)}, u32[]{:S(2)}) %collective-permute-start.33) | collective-permute-done | bytes 1056800 | tf_op jit(solution)/shard_map/ppermute | solution.py:69
  251.5 2.3 collective-permute-start.34
  256.1 3.3 %collective-permute-start.38 = (f32[512,256]{1,0:T(8,128)S(1)}, f32[512,256]{1,0:T(8,128)S(1)}, u32[]{:S(2)}, u32[]{:S(2)}) collective-permute-start(f32[512,256]{1,0:T(8,128)S(1)} %slice.44), channel_id=1, source_target_pairs={{0,12},{1,13},{2,14},{3,15},{4,0},{5,1},{6,2},{7,3},{8,4},{9,5},{1... | collective-permute-start | bytes 1572872 | tf_op jit(solution)/shard_map/ppermute | solution.py:69
  259.4 7.1 %collective-permute-done.34.refs_0_ = f32[1032,256]{1,0:T(8,128)S(1)} collective-permute-done((f32[1032,256]{1,0:T(8,128)S(1)}, f32[1032,256]{1,0:T(8,128)S(1)}, u32[]{:S(2)}, u32[]{:S(2)}) %collective-permute-start.34) | collective-permute-done | bytes 1056800 | tf_op jit(solution)/shard_map/ppermute | solution.py:69
  266.5 3.5 %collective-permute-start.35 = (f32[512,256]{1,0:T(8,128)S(1)}, f32[512,256]{1,0:T(8,128)S(1)}, u32[]{:S(2)}, u32[]{:S(2)}) collective-permute-start(f32[512,256]{1,0:T(8,128)S(1)} %slice.42), channel_id=1, source_target_pairs={{0,12},{1,13},{2,14},{3,15},{4,0},{5,1},{6,2},{7,3},{8,4},{9,5},{1... | collective-permute-start | bytes 1572872 | tf_op jit(solution)/shard_map/ppermute | solution.py:69
  270.2 4.8 %back_project.6.refs_6_ = f32[1024,256]{1,0:T(8,128)S(1)} custom-call(f32[1032,256]{1,0:T(8,128)S(1)} %lay.2.refs_0_, bf16[4,2,1024,512]{3,2,1,0:T(8,128)(2,1)} %get-tuple-element.49.refs_1_.refs_2_.refs_4_, bf16[4,2,1024,512]{3,2,1,0:T(8,128)(2,1)} %get-tuple-element.50.refs_2_.refs_3_.refs_5_), custom_call_target="tpu_custom_call" | custom-call | flops 25165824 | bytes 114688 | tf_op jit(solution)/shard_map/back_project/pallas_call | solution.py:44
  276.7 6.8 %back_project.7.refs_4_ = f32[1024,256]{1,0:T(8,128)S(1)} custom-call(f32[1032,256]{1,0:T(8,128)S(1)} %copy-done.8, f32[1032,256]{1,0:T(8,128)} %copy-done.19, bf16[4,2,1024,512]{3,2,1,0:T(8,128)(2,1)} %get-tuple-element.49.refs_1_.refs_2_.refs_4_, bf16[4,2,1024,512]{3,2,1,0:T(8,128)(2,1)} %get-tuple-element.50.refs_2_.refs_3_.refs_5_, ...), custom_call_target="tpu_custom_call" | custom-call | flops 50331648 | bytes 196608 | tf_op jit(solution)/shard_map/back_project/pallas_call | solution.py:44
  284.3 4.5 %back_project.8 = (f32[1024,128]{1,0:T(8,128)S(1)}, f32[1024,128]{1,0:T(8,128)S(1)}) custom-call(f32[512,256]{1,0:T(8,128)S(1)} %collective-permute-done.38.refs_0_, f32[520,256]{1,0:T(8,128)S(1)} %collective-permute-done.39.refs_1_, bf16[4,2,1024,512]{3,2,1,0:T(8,128)(2,1)} %get-tuple-element.49.refs_1_.refs_2_.refs_4_, ...), custom_call_target="tpu_custom_call" | custom-call | flops 25165824 | bytes 114688 | tf_op jit(solution)/shard_map/back_project/pallas_call | solution.py:44
  290.0 2.6 collective-permute-start.43
  292.6 4.4 %back_project.9.refs_6_ = f32[1024,256]{1,0:T(8,128)S(1)} custom-call(f32[1032,256]{1,0:T(8,128)S(1)} %copy-done.6, bf16[4,2,1024,512]{3,2,1,0:T(8,128)(2,1)} %get-tuple-element.49.refs_1_.refs_2_.refs_4_, bf16[4,2,1024,512]{3,2,1,0:T(8,128)(2,1)} %get-tuple-element.50.refs_2_.refs_3_.refs_5_, f32[1024,128]{1,0:T(8,128)S(1)} %get-tuple-element.81.refs_3_), custom_call_target="tpu_custom_call" | custom-call | flops 25165824 | bytes 114688 | tf_op jit(solution)/shard_map/back_project/pallas_call | solution.py:44
  297.6 6.8 %back_project.10.refs_4_ = f32[1024,256]{1,0:T(8,128)S(1)} custom-call(f32[1032,256]{1,0:T(8,128)S(1)} %collective-permute-done.34.refs_0_, f32[1032,256]{1,0:T(8,128)} %copy-done.22, bf16[4,2,1024,512]{3,2,1,0:T(8,128)(2,1)} %get-tuple-element.49.refs_1_.refs_2_.refs_4_, bf16[4,2,1024,512]{3,2,1,0:T(8,128)(2,1)} %get-tuple-element.50.refs_2_.refs_3_.refs_5_, ...), custom_call_target="tpu_custom_call" | custom-call | flops 50331648 | bytes 196608 | tf_op jit(solution)/shard_map/back_project/pallas_call | solution.py:44
  304.5 4.5 %back_project.11 = (f32[1024,128]{1,0:T(8,128)S(1)}, f32[1024,128]{1,0:T(8,128)S(1)}) custom-call(f32[512,256]{1,0:T(8,128)S(1)} %collective-permute-done.35.refs_0_, f32[512,256]{1,0:T(8,128)S(1)} %collective-permute-done.37.refs_1_, bf16[4,2,1024,512]{3,2,1,0:T(8,128)(2,1)} %get-tuple-element.49.refs_1_.refs_2_.refs_4_, ...), custom_call_target="tpu_custom_call" | custom-call | flops 25165824 | bytes 114688 | tf_op jit(solution)/shard_map/back_project/pallas_call | solution.py:44
  311.2 10.0 %collective-permute-done.44 = f32[1024,128]{1,0:T(8,128)} collective-permute-done((f32[1024,128]{1,0:T(8,128)S(1)}, f32[1024,128]{1,0:T(8,128)}, u32[]{:S(2)}, u32[]{:S(2)}) %collective-permute-start.44) | collective-permute-done | bytes 524320 | tf_op jit(solution)/shard_map/ppermute | solution.py:69
  (130 shorter events, 49.4 us)
Async XLA Ops:
  0.6 14.9 %collective-permute-start.5 = (f32[1024,2048]{1,0:T(8,128)}, f32[1024,2048]{1,0:T(8,128)}, u32[]{:S(2)}, u32[]{:S(2)}) collective-permute-start(f32[1024,2048]{1,0:T(8,128)} %refs_1_.4), channel_id=1, source_target_pairs={{0,16},{1,17},{2,18},{3,19},{4,20},{5,21},{6,22},{7,23},{8,24},{9,... | collective-permute-start | bytes 25165832 | tf_op jit(solution)/shard_map/ppermute | solution.py:69
  4.4 11.1 %collective-permute-start = (f32[128,1024]{1,0:T(8,128)S(1)}, f32[128,1024]{1,0:T(8,128)S(1)}, u32[]{:S(2)}, u32[]{:S(2)}) collective-permute-start(f32[128,1024]{1,0:T(8,128)S(1)} %get-tuple-element.46), channel_id=1, source_target_pairs={{0,16},{1,17},{2,18},{3,19},{4,20},{5,21},{6,22},{7,23},{8,24},{9,... | collective-permute-start | bytes 1572872 | tf_op jit(solution)/shard_map/ppermute | solution.py:69
  15.5 19.8 %copy-start.3 = (f32[256,1024]{1,0:T(8,128)}, f32[256,1024]{1,0:T(8,128)S(1)}, u32[]{:S(2)}) copy-start(f32[256,1024]{1,0:T(8,128)S(1)} %constant_dynamic-update-slice_fusion.refs_0_) | copy-start | bytes 3145732
  29.1 10.5 %collective-permute-start.6 = (f32[256,512]{1,0:T(8,128)S(1)}, f32[256,512]{1,0:T(8,128)S(1)}, u32[]{:S(2)}, u32[]{:S(2)}) collective-permute-start(f32[256,512]{1,0:T(8,128)S(1)} %get-tuple-element.51.refs_5_), channel_id=1, source_target_pairs={{0,4},{1,5},{2,6},{3,7},{4,8},{5,9},{6,10},{7,11},{8,12},{9,13},{1... | collective-permute-start | bytes 1572872 | tf_op jit(solution)/shard_map/ppermute | solution.py:69
  30.8 9.2 %collective-permute-start.7 = (f32[256,512]{1,0:T(8,128)S(1)}, f32[256,512]{1,0:T(8,128)S(1)}, u32[]{:S(2)}, u32[]{:S(2)}) collective-permute-start(f32[256,512]{1,0:T(8,128)S(1)} %get-tuple-element.52), channel_id=1, source_target_pairs={{0,12},{1,13},{2,14},{3,15},{4,0},{5,1},{6,2},{7,3},{8,4},{9,5},{1... | collective-permute-start | bytes 1572872 | tf_op jit(solution)/shard_map/ppermute | solution.py:69
  32.4 26.1 %collective-permute-start.1 = (f32[256,1024]{1,0:T(8,128)S(1)}, f32[256,1024]{1,0:T(8,128)S(1)}, u32[]{:S(2)}, u32[]{:S(2)}) collective-permute-start(f32[256,1024]{1,0:T(8,128)S(1)} %constant_dynamic-update-slice_fusion.refs_0_), channel_id=1, source_target_pairs={{0,96},{1,97},{2,98},{3,99},{4,100},{5,101},{6,102},{7,103},{8,104... | collective-permute-start | bytes 3145736 | tf_op jit(solution)/shard_map/ppermute | solution.py:69
  35.3 26.6 %collective-permute-start.3 = (f32[256,1024]{1,0:T(8,128)S(1)}, f32[256,1024]{1,0:T(8,128)S(1)}, u32[]{:S(2)}, u32[]{:S(2)}) collective-permute-start(f32[256,1024]{1,0:T(8,128)S(1)} %constant_dynamic-update-slice_fusion.refs_0_), channel_id=1, source_target_pairs={{0,32},{1,33},{2,34},{3,35},{4,36},{5,37},{6,38},{7,39},{8,40},{9,... | collective-permute-start | bytes 3145736 | tf_op jit(solution)/shard_map/ppermute | solution.py:69
  47.0 14.9 %copy-start.12 = (f32[256,1024]{1,0:T(8,128)}, f32[256,1024]{1,0:T(8,128)S(1)}, u32[]{:S(2)}) copy-start(f32[256,1024]{1,0:T(8,128)S(1)} %get-tuple-element.53.refs_4_) | copy-start | bytes 3145732
  47.0 26.6 %collective-permute-start.8 = (f32[256,1024]{1,0:T(8,128)S(1)}, f32[256,1024]{1,0:T(8,128)S(1)}, u32[]{:S(2)}, u32[]{:S(2)}) collective-permute-start(f32[256,1024]{1,0:T(8,128)S(1)} %get-tuple-element.53.refs_4_), channel_id=1, source_target_pairs={{0,4},{1,5},{2,6},{3,7},{4,8},{5,9},{6,10},{7,11},{8,12},{9,13},{1... | collective-permute-start | bytes 3145736 | tf_op jit(solution)/shard_map/ppermute | solution.py:69
  48.7 26.8 %collective-permute-start.9 = (f32[256,1024]{1,0:T(8,128)S(1)}, f32[256,1024]{1,0:T(8,128)S(1)}, u32[]{:S(2)}, u32[]{:S(2)}) collective-permute-start(f32[256,1024]{1,0:T(8,128)S(1)} %get-tuple-element.54), channel_id=1, source_target_pairs={{0,12},{1,13},{2,14},{3,15},{4,0},{5,1},{6,2},{7,3},{8,4},{9,5},{1... | collective-permute-start | bytes 3145736 | tf_op jit(solution)/shard_map/ppermute | solution.py:69
  68.8 22.7 %collective-permute-start.12 = (f32[512,512]{1,0:T(8,128)S(1)}, f32[512,512]{1,0:T(8,128)S(1)}, u32[]{:S(2)}, u32[]{:S(2)}) collective-permute-start(f32[512,512]{1,0:T(8,128)S(1)} %get-tuple-element.55.refs_7_), channel_id=1, source_target_pairs={{0,4},{1,5},{2,6},{3,7},{4,8},{5,9},{6,10},{7,11},{8,12},{9,13},{1... | collective-permute-start | bytes 3145736 | tf_op jit(solution)/shard_map/ppermute | solution.py:69
  69.4 22.2 %collective-permute-start.13 = (f32[512,512]{1,0:T(8,128)S(1)}, f32[512,512]{1,0:T(8,128)S(1)}, u32[]{:S(2)}, u32[]{:S(2)}) collective-permute-start(f32[512,512]{1,0:T(8,128)S(1)} %get-tuple-element.59), channel_id=1, source_target_pairs={{0,12},{1,13},{2,14},{3,15},{4,0},{5,1},{6,2},{7,3},{8,4},{9,5},{1... | collective-permute-start | bytes 3145736 | tf_op jit(solution)/shard_map/ppermute | solution.py:69
  72.2 12.9 %collective-permute-start.2 = (f32[128,1024]{1,0:T(8,128)S(1)}, f32[128,1024]{1,0:T(8,128)S(1)}, u32[]{:S(2)}, u32[]{:S(2)}) collective-permute-start(f32[128,1024]{1,0:T(8,128)S(1)} %slice.40), channel_id=1, source_target_pairs={{0,96},{1,97},{2,98},{3,99},{4,100},{5,101},{6,102},{7,103},{8,104... | collective-permute-start | bytes 1572872 | tf_op jit(solution)/shard_map/ppermute | solution.py:69
  73.6 14.0 %collective-permute-start.4 = (f32[128,1024]{1,0:T(8,128)S(1)}, f32[128,1024]{1,0:T(8,128)S(1)}, u32[]{:S(2)}, u32[]{:S(2)}) collective-permute-start(f32[128,1024]{1,0:T(8,128)S(1)} %slice.41), channel_id=1, source_target_pairs={{0,32},{1,33},{2,34},{3,35},{4,36},{5,37},{6,38},{7,39},{8,40},{9,... | collective-permute-start | bytes 1572872 | tf_op jit(solution)/shard_map/ppermute | solution.py:69
  103.8 43.9 %collective-permute-start.16 = (f32[512,1024]{1,0:T(8,128)}, f32[512,1024]{1,0:T(8,128)S(1)}, u32[]{:S(2)}, u32[]{:S(2)}) collective-permute-start(f32[512,1024]{1,0:T(8,128)} %get-tuple-element.60.refs_6_), channel_id=1, source_target_pairs={{0,4},{1,5},{2,6},{3,7},{4,8},{5,9},{6,10},{7,11},{8,12},{9,13},{1... | collective-permute-start | bytes 6291464 | tf_op jit(solution)/shard_map/ppermute | solution.py:69
  104.8 42.9 %collective-permute-start.17 = (f32[512,1024]{1,0:T(8,128)}, f32[512,1024]{1,0:T(8,128)}, u32[]{:S(2)}, u32[]{:S(2)}) collective-permute-start(f32[512,1024]{1,0:T(8,128)} %get-tuple-element.63), channel_id=1, source_target_pairs={{0,12},{1,13},{2,14},{3,15},{4,0},{5,1},{6,2},{7,3},{8,4},{9,5},{1... | collective-permute-start | bytes 6291464 | tf_op jit(solution)/shard_map/ppermute | solution.py:69
  107.1 29.8 %collective-permute-start.10 = (f32[256,512]{1,0:T(8,128)S(1)}, f32[256,512]{1,0:T(8,128)S(1)}, u32[]{:S(2)}, u32[]{:S(2)}) collective-permute-start(f32[256,512]{1,0:T(8,128)S(1)} %get-tuple-element.57.refs_6_), channel_id=1, source_target_pairs={{0,4},{1,5},{2,6},{3,7},{4,8},{5,9},{6,10},{7,11},{8,12},{9,13},{1... | collective-permute-start | bytes 1572872 | tf_op jit(solution)/shard_map/ppermute | solution.py:69
  107.1 29.8 %collective-permute-start.11 = (f32[256,512]{1,0:T(8,128)S(1)}, f32[256,512]{1,0:T(8,128)S(1)}, u32[]{:S(2)}, u32[]{:S(2)}) collective-permute-start(f32[256,512]{1,0:T(8,128)S(1)} %get-tuple-element.58), channel_id=1, source_target_pairs={{0,12},{1,13},{2,14},{3,15},{4,0},{5,1},{6,2},{7,3},{8,4},{9,5},{1... | collective-permute-start | bytes 1572872 | tf_op jit(solution)/shard_map/ppermute | solution.py:69
  144.4 21.7 %collective-permute-start.14 = (f32[256,1024]{1,0:T(8,128)S(1)}, f32[256,1024]{1,0:T(8,128)S(1)}, u32[]{:S(2)}, u32[]{:S(2)}) collective-permute-start(f32[256,1024]{1,0:T(8,128)S(1)} %get-tuple-element.61.refs_8_), channel_id=1, source_target_pairs={{0,4},{1,5},{2,6},{3,7},{4,8},{5,9},{6,10},{7,11},{8,12},{9,13},{1... | collective-permute-start | bytes 3145736 | tf_op jit(solution)/shard_map/ppermute | solution.py:69
  145.8 20.4 %collective-permute-start.15 = (f32[256,1024]{1,0:T(8,128)}, f32[256,1024]{1,0:T(8,128)S(1)}, u32[]{:S(2)}, u32[]{:S(2)}) collective-permute-start(f32[256,1024]{1,0:T(8,128)} %get-tuple-element.62), channel_id=1, source_target_pairs={{0,12},{1,13},{2,14},{3,15},{4,0},{5,1},{6,2},{7,3},{8,4},{9,5},{1... | collective-permute-start | bytes 3145736 | tf_op jit(solution)/shard_map/ppermute | solution.py:69
  147.7 12.9 %collective-permute-start.24 = (f32[256,256]{1,0:T(8,128)S(1)}, f32[256,256]{1,0:T(8,128)S(1)}, u32[]{:S(2)}, u32[]{:S(2)}) collective-permute-start(f32[256,256]{1,0:T(8,128)S(1)} %get-tuple-element.74), channel_id=1, source_target_pairs={{0,1},{1,2},{2,3},{3,0},{4,5},{5,6},{6,7},{7,4},{8,9},{9,10},{10,1... | collective-permute-start | bytes 786440 | tf_op jit(solution)/shard_map/ppermute | solution.py:69
  157.3 25.9 %collective-permute-start.21 = (f32[512,256]{1,0:T(8,128)S(1)}, f32[512,256]{1,0:T(8,128)S(1)}, u32[]{:S(2)}, u32[]{:S(2)}) collective-permute-start(f32[512,256]{1,0:T(8,128)S(1)} %get-tuple-element.71), channel_id=1, source_target_pairs={{0,1},{1,2},{2,3},{3,0},{4,5},{5,6},{6,7},{7,4},{8,9},{9,10},{10,1... | collective-permute-start | bytes 1572872 | tf_op jit(solution)/shard_map/ppermute | solution.py:69
  157.3 40.9 %collective-permute-start.22 = (f32[512,256]{1,0:T(8,128)}, f32[512,256]{1,0:T(8,128)S(1)}, u32[]{:S(2)}, u32[]{:S(2)}) collective-permute-start(f32[512,256]{1,0:T(8,128)} %get-tuple-element.72), channel_id=1, source_target_pairs={{0,3},{1,0},{2,1},{3,2},{4,7},{5,4},{6,5},{7,6},{8,11},{9,8},{10,9... | collective-permute-start | bytes 1572872 | tf_op jit(solution)/shard_map/ppermute | solution.py:69
  160.6 37.6 %collective-permute-start.23 = (f32[512,256]{1,0:T(8,128)}, f32[512,256]{1,0:T(8,128)S(1)}, u32[]{:S(2)}, u32[]{:S(2)}) collective-permute-start(f32[512,256]{1,0:T(8,128)} %get-tuple-element.73), channel_id=1, source_target_pairs={{0,2},{1,3},{2,0},{3,1},{4,6},{5,7},{6,4},{7,5},{8,10},{9,11},{10,... | collective-permute-start | bytes 1572872 | tf_op jit(solution)/shard_map/ppermute | solution.py:69
  166.1 12.7 %collective-permute-start.25 = (f32[256,256]{1,0:T(8,128)S(1)}, f32[256,256]{1,0:T(8,128)S(1)}, u32[]{:S(2)}, u32[]{:S(2)}) collective-permute-start(f32[256,256]{1,0:T(8,128)S(1)} %get-tuple-element.75), channel_id=1, source_target_pairs={{0,3},{1,0},{2,1},{3,2},{4,7},{5,4},{6,5},{7,6},{8,11},{9,8},{10,9... | collective-permute-start | bytes 786440 | tf_op jit(solution)/shard_map/ppermute | solution.py:69
  166.1 12.7 %collective-permute-start.26 = (f32[256,256]{1,0:T(8,128)S(1)}, f32[256,256]{1,0:T(8,128)S(1)}, u32[]{:S(2)}, u32[]{:S(2)}) collective-permute-start(f32[256,256]{1,0:T(8,128)S(1)} %get-tuple-element.76), channel_id=1, source_target_pairs={{0,2},{1,3},{2,0},{3,1},{4,6},{5,7},{6,4},{7,5},{8,10},{9,11},{10,... | collective-permute-start | bytes 786440 | tf_op jit(solution)/shard_map/ppermute | solution.py:69
  178.8 23.6 %collective-permute-start.18 = (f32[256,256]{1,0:T(8,128)}, f32[256,256]{1,0:T(8,128)S(1)}, u32[]{:S(2)}, u32[]{:S(2)}) collective-permute-start(f32[256,256]{1,0:T(8,128)} %get-tuple-element.66), channel_id=1, source_target_pairs={{0,1},{1,2},{2,3},{3,0},{4,5},{5,6},{6,7},{7,4},{8,9},{9,10},{10,1... | collective-permute-start | bytes 786440 | tf_op jit(solution)/shard_map/ppermute | solution.py:69
  179.5 22.9 %collective-permute-start.19 = (f32[256,256]{1,0:T(8,128)}, f32[256,256]{1,0:T(8,128)}, u32[]{:S(2)}, u32[]{:S(2)}) collective-permute-start(f32[256,256]{1,0:T(8,128)} %get-tuple-element.67), channel_id=1, source_target_pairs={{0,3},{1,0},{2,1},{3,2},{4,7},{5,4},{6,5},{7,6},{8,11},{9,8},{10,9... | collective-permute-start | bytes 786440 | tf_op jit(solution)/shard_map/ppermute | solution.py:69
  183.2 19.2 %collective-permute-start.20 = (f32[256,256]{1,0:T(8,128)}, f32[256,256]{1,0:T(8,128)}, u32[]{:S(2)}, u32[]{:S(2)}) collective-permute-start(f32[256,256]{1,0:T(8,128)} %get-tuple-element.68), channel_id=1, source_target_pairs={{0,2},{1,3},{2,0},{3,1},{4,6},{5,7},{6,4},{7,5},{8,10},{9,11},{10,... | collective-permute-start | bytes 786440 | tf_op jit(solution)/shard_map/ppermute | solution.py:69
  206.2 2.0 collective-permute-start.27
  213.9 1.6 collective-permute-start.28
  215.5 9.6 %collective-permute-start.29 = (f32[2,136,512]{2,1,0:T(8,128)S(1)}, f32[2,136,512]{2,1,0:T(8,128)S(1)}, u32[]{:S(2)}, u32[]{:S(2)}) collective-permute-start(f32[2,136,512]{2,1,0:T(8,128)S(1)} %pad_maximum_fusion.refs_0_), channel_id=1, source_target_pairs={{0,3},{1,0},{2,1},{3,2},{4,7},{5,4},{6,5},{7,6},{8,11},{9,8},{10,9... | collective-permute-start | bytes 1671176 | tf_op jit(solution)/shard_map/ppermute | solution.py:69
  216.2 11.1 %collective-permute-start.30 = (f32[2,136,512]{2,1,0:T(8,128)S(1)}, f32[2,136,512]{2,1,0:T(8,128)S(1)}, u32[]{:S(2)}, u32[]{:S(2)}) collective-permute-start(f32[2,136,512]{2,1,0:T(8,128)S(1)} %pad_maximum_fusion.refs_0_), channel_id=1, source_target_pairs={{0,2},{1,3},{2,0},{3,1},{4,6},{5,7},{6,4},{7,5},{8,10},{9,11},{10,... | collective-permute-start | bytes 1671176 | tf_op jit(solution)/shard_map/ppermute | solution.py:69
  218.9 14.3 %collective-permute-start.31 = (f32[2,136,512]{2,1,0:T(8,128)S(1)}, f32[2,136,512]{2,1,0:T(8,128)S(1)}, u32[]{:S(2)}, u32[]{:S(2)}) collective-permute-start(f32[2,136,512]{2,1,0:T(8,128)S(1)} %pad_maximum_fusion.refs_0_), channel_id=1, source_target_pairs={{0,1},{1,2},{2,3},{3,0},{4,5},{5,6},{6,7},{7,4},{8,9},{9,10},{10,1... | collective-permute-start | bytes 1671176 | tf_op jit(solution)/shard_map/ppermute | solution.py:69
  233.3 16.2 %collective-permute-start.33 = (f32[1032,256]{1,0:T(8,128)S(1)}, f32[1032,256]{1,0:T(8,128)S(1)}, u32[]{:S(2)}, u32[]{:S(2)}) collective-permute-start(f32[1032,256]{1,0:T(8,128)S(1)} %lay.2.refs_0_), channel_id=1, source_target_pairs={{0,4},{1,5},{2,6},{3,7},{4,8},{5,9},{6,10},{7,11},{8,12},{9,13},{1... | collective-permute-start | bytes 3170312 | tf_op jit(solution)/shard_map/ppermute | solution.py:69
  233.4 16.0 %collective-permute-start.32 = (f32[1032,256]{1,0:T(8,128)S(1)}, f32[1032,256]{1,0:T(8,128)S(1)}, u32[]{:S(2)}, u32[]{:S(2)}) collective-permute-start(f32[1032,256]{1,0:T(8,128)S(1)} %lay.2.refs_0_), channel_id=1, source_target_pairs={{0,12},{1,13},{2,14},{3,15},{4,0},{5,1},{6,2},{7,3},{8,4},{9,5},{1... | collective-permute-start | bytes 3170312 | tf_op jit(solution)/shard_map/ppermute | solution.py:69
  251.5 18.6 %copy-start.5 = (f32[1032,256]{1,0:T(8,128)}, f32[1032,256]{1,0:T(8,128)S(1)}, u32[]{:S(2)}) copy-start(f32[1032,256]{1,0:T(8,128)S(1)} %lay.3.refs_7_.refs_0_) | copy-start | bytes 3170308
  251.5 15.0 %collective-permute-start.34 = (f32[1032,256]{1,0:T(8,128)S(1)}, f32[1032,256]{1,0:T(8,128)S(1)}, u32[]{:S(2)}, u32[]{:S(2)}) collective-permute-start(f32[1032,256]{1,0:T(8,128)S(1)} %lay.3.refs_7_.refs_0_), channel_id=1, source_target_pairs={{0,12},{1,13},{2,14},{3,15},{4,0},{5,1},{6,2},{7,3},{8,4},{9,5},{1... | collective-permute-start | bytes 3170312 | tf_op jit(solution)/shard_map/ppermute | solution.py:69
  253.9 16.2 %collective-permute-start.36 = (f32[1032,256]{1,0:T(8,128)S(1)}, f32[1032,256]{1,0:T(8,128)S(1)}, u32[]{:S(2)}, u32[]{:S(2)}) collective-permute-start(f32[1032,256]{1,0:T(8,128)S(1)} %lay.3.refs_7_.refs_0_), channel_id=1, source_target_pairs={{0,4},{1,5},{2,6},{3,7},{4,8},{5,9},{6,10},{7,11},{8,12},{9,13},{1... | collective-permute-start | bytes 3170312 | tf_op jit(solution)/shard_map/ppermute | solution.py:69
  255.0 20.7 %collective-permute-start.39 = (f32[520,256]{1,0:T(8,128)S(1)}, f32[520,256]{1,0:T(8,128)S(1)}, u32[]{:S(2)}, u32[]{:S(2)}) collective-permute-start(f32[520,256]{1,0:T(8,128)S(1)} %slice.45), channel_id=1, source_target_pairs={{0,4},{1,5},{2,6},{3,7},{4,8},{5,9},{6,10},{7,11},{8,12},{9,13},{1... | collective-permute-start | bytes 1597448 | tf_op jit(solution)/shard_map/ppermute | solution.py:69
  256.1 28.2 %collective-permute-start.38 = (f32[512,256]{1,0:T(8,128)S(1)}, f32[512,256]{1,0:T(8,128)S(1)}, u32[]{:S(2)}, u32[]{:S(2)}) collective-permute-start(f32[512,256]{1,0:T(8,128)S(1)} %slice.44), channel_id=1, source_target_pairs={{0,12},{1,13},{2,14},{3,15},{4,0},{5,1},{6,2},{7,3},{8,4},{9,5},{1... | collective-permute-start | bytes 1572872 | tf_op jit(solution)/shard_map/ppermute | solution.py:69
  266.5 37.9 %collective-permute-start.35 = (f32[512,256]{1,0:T(8,128)S(1)}, f32[512,256]{1,0:T(8,128)S(1)}, u32[]{:S(2)}, u32[]{:S(2)}) collective-permute-start(f32[512,256]{1,0:T(8,128)S(1)} %slice.42), channel_id=1, source_target_pairs={{0,12},{1,13},{2,14},{3,15},{4,0},{5,1},{6,2},{7,3},{8,4},{9,5},{1... | collective-permute-start | bytes 1572872 | tf_op jit(solution)/shard_map/ppermute | solution.py:69
  270.1 34.3 %collective-permute-start.37 = (f32[512,256]{1,0:T(8,128)S(1)}, f32[512,256]{1,0:T(8,128)S(1)}, u32[]{:S(2)}, u32[]{:S(2)}) collective-permute-start(f32[512,256]{1,0:T(8,128)S(1)} %slice.43), channel_id=1, source_target_pairs={{0,4},{1,5},{2,6},{3,7},{4,8},{5,9},{6,10},{7,11},{8,12},{9,13},{1... | collective-permute-start | bytes 1572872 | tf_op jit(solution)/shard_map/ppermute | solution.py:69
  276.4 7.1 %collective-permute-start.40 = (f32[8,128]{1,0:T(8,128)S(1)}, f32[8,128]{1,0:T(8,128)S(1)}, u32[]{:S(2)}, u32[]{:S(2)}) collective-permute-start(f32[8,128]{1,0:T(8,128)S(1)} %fusion), channel_id=1, source_target_pairs={{0,32},{1,33},{2,34},{3,35},{4,36},{5,37},{6,38},{7,39},{8,40},{9,... | collective-permute-start | bytes 12296 | tf_op jit(solution)/shard_map/ppermute | solution.py:69
  283.5 13.5 %collective-permute-start.41 = (f32[8,128]{1,0:T(8,128)S(1)}, f32[8,128]{1,0:T(8,128)S(1)}, u32[]{:S(2)}, u32[]{:S(2)}) collective-permute-start(f32[8,128]{1,0:T(8,128)S(1)} %add.48), channel_id=1, source_target_pairs={{0,64},{1,65},{2,66},{3,67},{4,68},{5,69},{6,70},{7,71},{8,72},{9,... | collective-permute-start | bytes 12296 | tf_op jit(solution)/shard_map/ppermute | solution.py:69
  288.8 22.4 %collective-permute-start.42 = (f32[1024,128]{1,0:T(8,128)S(1)}, f32[1024,128]{1,0:T(8,128)S(1)}, u32[]{:S(2)}, u32[]{:S(2)}) collective-permute-start(f32[1024,128]{1,0:T(8,128)S(1)} %get-tuple-element.81.refs_3_), channel_id=1, source_target_pairs={{0,32},{1,33},{2,34},{3,35},{4,36},{5,37},{6,38},{7,39},{8,40},{9,... | collective-permute-start | bytes 1572872 | tf_op jit(solution)/shard_map/ppermute | solution.py:69
  290.0 21.2 %collective-permute-start.43 = (f32[1024,128]{1,0:T(8,128)S(1)}, f32[1024,128]{1,0:T(8,128)S(1)}, u32[]{:S(2)}, u32[]{:S(2)}) collective-permute-start(f32[1024,128]{1,0:T(8,128)S(1)} %get-tuple-element.83), channel_id=1, source_target_pairs={{0,96},{1,97},{2,98},{3,99},{4,100},{5,101},{6,102},{7,103},{8,104... | collective-permute-start | bytes 1572872 | tf_op jit(solution)/shard_map/ppermute | solution.py:69
  308.9 12.2 %collective-permute-start.44 = (f32[1024,128]{1,0:T(8,128)S(1)}, f32[1024,128]{1,0:T(8,128)}, u32[]{:S(2)}, u32[]{:S(2)}) collective-permute-start(f32[1024,128]{1,0:T(8,128)S(1)} %get-tuple-element.84), channel_id=1, source_target_pairs={{0,64},{1,65},{2,66},{3,67},{4,68},{5,69},{6,70},{7,71},{8,72},{9,... | collective-permute-start | bytes 1572872 | tf_op jit(solution)/shard_map/ppermute | solution.py:69
  (21 other events, 69.2 us)
